TPU v7x, 1024 devices: a whole 8x8x8 slice. The times are simulated.
1024 devices in a mesh: depth: 8 (over x), row: 8 (over y_lo, core), col: 16 (over y_hi, z).
Axes of the slice: x: 8, y: 8 (y_hi: 2, y_lo: 4; y = y_hi * 4 + y_lo), z: 8, core: 2. Of those that a mesh axis runs over, the one named last changes fastest.
Arguments:
- matrix_tiles: bfloat16 [2048, 256, 256], P(('depth', 'row', 'col')), may hold values from -3 to 3
- matrix_where: int32 [2048, 2], P(('depth', 'row', 'col')), may hold values from 0 to 511, as said below
- matrix_count: int32 [1024], P(('depth', 'row', 'col')), may hold values from 0 to 2, as said below
- square_tiles: bfloat16 [4096, 256, 256], P(('depth', 'row', 'col')), may hold values from -0.375 to 0.375
- square_where: int32 [4096, 2], P(('depth', 'row', 'col')), may hold values from 0 to 511, as said below
- square_count: int32 [1024], P(('depth', 'row', 'col')), may hold values from 0 to 4, as said below
Outputs:
- sign_step: float32 [2048, 4096], P('row', 'col')
Inputs may be any that keep to these rules, and one draw needn't show every extreme that they name: `matrix_count`: among the devices that share a depth and a row index, at least one has exactly 2 live slots. `matrix_where`: every slot of the device at depth d, row r, col c names block row r and inner block d * 64 + c * 4 + s for some 0 <= s < 4; the slots of one device name distinct blocks. `square_count`: among the devices that share a depth and a col index, at least one has exactly 4 live slots. `square_where`: every slot of the device at depth d, row r, col c names inner block d * 64 + r * 8 + s for some 0 <= s < 8 and block column c; the slots of one device name distinct blocks.
All inputs are finite; a program needn't handle non-finite values.
Results may differ from a plain program's by a relative error of at most 0.0003.
Values may be sent and summed in bfloat16 or wider, within the bound.
No kernel may reach another device: no remote copies, remote signals or barrier semaphores. Data moves between devices by JAX's collectives and lax.ppermute only.
A program may use at most 64 MiB of HBM per device.

v0:
```python
import jax
import jax.numpy as jnp
from jax import lax
from jax.sharding import PartitionSpec as P

KDEP = 64


def place_slab(tiles, positions, slab_size):
    select_mask = (positions[None, :] == jnp.arange(slab_size, dtype=jnp.int32)[:, None]).astype(
        jnp.bfloat16
    )
    placed = jnp.einsum("sn,nab->sab", select_mask, tiles, preferred_element_type=jnp.float32)
    return placed.astype(jnp.bfloat16)


def block_update(piece_tiles, square_rows, inner_keys, inner_base, col_at):
    product = jnp.einsum(
        "nab,nbc->ac", piece_tiles, square_rows, preferred_element_type=jnp.float32
    )
    on_diagonal = (inner_keys + inner_base == col_at) & (inner_keys >= 0)
    diagonal_part = jnp.einsum(
        "n,nab->ab",
        on_diagonal.astype(jnp.bfloat16),
        piece_tiles,
        preferred_element_type=jnp.float32,
    )
    return 1.5 * diagonal_part - 0.5 * product


def on_device(matrix_tiles, matrix_where, matrix_count, square_tiles, square_where, square_count):
    layer_at = lax.axis_index("depth")
    row_at = lax.axis_index("row")
    col_at = lax.axis_index("col")
    inner_base = layer_at * KDEP
    matrix_slots = matrix_tiles.shape[0]
    square_slots = square_tiles.shape[0]
    matrix_live = jnp.arange(matrix_slots, dtype=jnp.int32) < matrix_count[0]
    square_live = jnp.arange(square_slots, dtype=jnp.int32) < square_count[0]
    matrix_key = jnp.where(matrix_live, matrix_where[:, 1] - inner_base, -1)
    square_key = jnp.where(square_live, square_where[:, 0] - inner_base, -1)
    square_width = KDEP // lax.axis_size("row")
    square_own = place_slab(square_tiles, square_key - row_at * square_width, square_width)
    square_panel = lax.all_gather(square_own, "row", axis=0, tiled=True)
    matrix_width = KDEP // lax.axis_size("col")
    matrix_own = place_slab(matrix_tiles, matrix_key - col_at * matrix_width, matrix_width)
    shard_piece = lax.all_gather(matrix_own, "col", axis=0, tiled=True)
    piece_rows = shard_piece.shape[0]
    inner_keys = jnp.arange(piece_rows, dtype=jnp.int32)
    layer_part = block_update(shard_piece, square_panel, inner_keys, inner_base, col_at)
    return lax.psum(layer_part, "depth")


def solution(mesh):
    in_specs = (
        P(("depth", "row", "col"), None, None),
        P(("depth", "row", "col"), None),
        P(("depth", "row", "col")),
        P(("depth", "row", "col"), None, None),
        P(("depth", "row", "col"), None),
        P(("depth", "row", "col")),
    )
    out_specs = P("row", "col")
    return jax.shard_map(
        on_device, mesh=mesh, in_specs=in_specs, out_specs=out_specs, check_vma=False
    )
```

profile of v0, /device:TPU:2, one launch (start us, length us, event | category | flops | bytes accessed | tf_op | source)
XLA Modules:
  0.0 420.9 jit_solution(10568646192123601212)
XLA Ops:
  6.5 0.0 copy-start
  6.5 0.0 all-gather.3.cloned.1.call-start
  7.3 0.9 subtract_reduce_fusion
  8.1 1.5 convolution_convert_fusion
  9.7 0.9 copy.10
  10.6 0.0 all-gather.3.cloned.1.call-update
  10.6 0.0 all-gather.5.cloned.1.call-start
  11.3 0.7 fusion.16
  12.0 0.0 copy-done
  12.0 0.5 fusion.4
  12.4 1.2 copy.23
  13.6 0.0 all-gather.5.cloned.1.call-update
  13.6 0.0 all-reduce.2.cloned.1.call-start
  13.7 212.7 %all-gather.3.cloned.1.call-done = bf16[64,256,256]{2,1,0:T(8,128)(2,1)} async-done(((bf16[4,256,256]{2,1,0:T(8,128)(2,1)}), bf16[64,256,256]{2,1,0:T(8,128)(2,1)}) %all-gather.3.cloned.1.call-update) | async-done | bytes 8388624 | tf_op jit(solution)/shard_map/all_gather | solution.py:47
  226.4 8.0 %fusion = f32[1,256,256]{2,0,1:T(1,128)S(1)} fusion(bf16[64,256,256]{2,1,0:T(8,128)(2,1)} %all-gather.3.cloned.1.call-done, s32[]{:T(128)S(6)} %axis_index.35, s32[]{:T(128)S(6)} %mul.21), kind=kOutput, calls=%fused_computation | convolution fusion | flops 8388736 | bytes 8650760 | tf_op jit(solution)/shard_map/n,nab->ab/dot_general | solution.py:22
  234.4 86.7 %all-gather.5.cloned.1.call-done = bf16[64,256,256]{2,1,0:T(8,128)(2,1)} async-done(((bf16[8,256,256]{2,1,0:T(8,128)(2,1)}), bf16[64,256,256]{2,1,0:T(8,128)(2,1)}) %all-gather.5.cloned.1.call-update) | async-done | bytes 8388624 | tf_op jit(solution)/shard_map/all_gather | solution.py:44
  321.1 8.8 %fusion.3 = f32[256,256]{1,0:T(8,128)} fusion(bf16[64,256,256]{2,1,0:T(8,128)(2,1)} %all-gather.3.cloned.1.call-done, bf16[64,256,256]{2,1,0:T(8,128)(2,1)} %all-gather.5.cloned.1.call-done, f32[1,256,256]{2,0,1:T(1,128)S(1)} %fusion), kind=kOutput, calls=%fused_computation.6 | convolution fusion | flops 2147680256 | bytes 17301504 | tf_op jit(solution)/shard_map/nab,nbc->ac/dot_general | solution.py:18
  329.9 0.0 all-reduce.2.cloned.1.call-update
  329.9 82.8 %all-reduce.2.cloned.1.call-done = f32[256,256]{1,0:T(8,128)} async-done(((f32[256,256]{1,0:T(8,128)}), f32[256,256]{1,0:T(8,128)}) %all-reduce.2.cloned.1.call-update) | async-done | bytes 262160 | tf_op jit(solution)/shard_map/psum | solution.py:51
  412.7 1.7 copy.27
  (1 shorter events, 0.0 us)
Async XLA Ops:
  6.5 5.4 %copy-start = (bf16[4,256,256]{2,1,0:T(8,128)(2,1)S(1)}, bf16[4,256,256]{2,1,0:T(8,128)(2,1)}, u32[]{:S(2)}) copy-start(bf16[4,256,256]{2,1,0:T(8,128)(2,1)} %param.9) | copy-start | bytes 1572868
  6.5 219.9 %all-gather.3.cloned.1.call-start = ((), (), s32[]{:S(2)}) async-start(), calls=%async_computation | async-start | bytes 8912896 | tf_op jit(solution)/shard_map/all_gather | solution.py:47
  10.6 310.5 %all-gather.5.cloned.1.call-start = ((), (), s32[]{:S(2)}) async-start(), calls=%async_computation.1 | async-start | bytes 9437184 | tf_op jit(solution)/shard_map/all_gather | solution.py:44
  13.6 399.1 %all-reduce.2.cloned.1.call-start = ((), (), s32[]{:S(2)}) async-start(), calls=%async_computation.2 | async-start | bytes 524288 | tf_op jit(solution)/shard_map/psum | solution.py:51
Sparse Core Ops, SparseCore 0:
  11.7 214.6 all-gather.2
  229.1 91.9 all-gather.4
  330.0 82.6 all-reduce.1
where the time goes:
time: 421 us
  waiting for transfers between devices  382 us (91%)
  matrix products  18.8 us (4%)
  between operations  14.5 us (3%)
    all_gather x1, waiting for transfers between devices, on_device(): shard_piece = lax.all_gather(matrix_own, 'col', axis=0, tiled=True)  213 us
    all_gather x1, waiting for transfers between devices, on_device(): square_panel = lax.all_gather(square_own, 'row', axis=0, tiled=True)  86.7 us
    psum x1, waiting for transfers between devices, on_device(): return lax.psum(layer_part, 'depth')  82.8 us
    dot_general x1, matrix products, block_update(): jnp.einsum('nab,nbc->ac', piece_tiles, square_rows, preferred_element_typ...  8.8 us
  transfers between devices with their start and end apart: 3, of which 3 were waited for; matrix products, arithmetic and copies ran while one was open for 2% of the time, Pallas kernels for 0%

commit v1 on v0

v1 whole, which is shorter than its diff:
```python
import functools

import jax
import jax.numpy as jnp
from jax import lax
from jax.experimental import pallas as pl
from jax.experimental.pallas import tpu as pltpu
from jax.sharding import PartitionSpec as P

TILE = 256
META = 16
MSG = 2 * TILE + META
KDEP = 64
XSLAB = 4
QSLAB = 8
ROW_COL = ("row", "col")


def flat(y, core, z):
    return ((y & 3) * 2 + core) * 16 + (y >> 2) * 8 + z


def places():
    return [(y, core, z) for y in range(8) for core in range(2) for z in range(8)]


def core_pairs():
    return [
        (flat(y, 1 - core, z), flat(y, core, z)) for y, core, z in places() if (z >> 1 & 1) == core
    ]


def swap_pairs():
    return [(flat(y, core, z), flat(y, 1 - core, z)) for y, core, z in places()]


def z_pairs(step, way):
    pairs = []
    for y, core, z in places():
        origin = (z - way * (step - 1)) % 8
        if (origin >> 1 & 1) == core:
            pairs.append((flat(y, core, z), flat(y, core, (z + way) % 8)))
    return pairs


def y_pairs(step, way, reach):
    pairs = []
    for y, core, z in places():
        origin = (y - way * (step - 1)) % 8
        ends = [(origin + way * t) % 8 for t in range(step, reach + 1)]
        if any((origin >> 1 & 1) == (end >> 2) for end in ends):
            pairs.append((flat(y, core, z), flat((y + way) % 8, core, z)))
    return pairs


def with_keys(tiles, keys):
    rows = jnp.broadcast_to(jnp.pad(keys, (0, META - 2), constant_values=-1)[:, None], (META, TILE))
    return jnp.concatenate([tiles.reshape(2 * TILE, TILE), rows.astype(jnp.bfloat16)], axis=0)


def product_kernel(*refs):
    x_refs, qa_refs, qb_refs = refs[:8], refs[8:16], refs[16:24]
    keep_ref, send_ref, x_buf, q_buf, key_vec, keys, x_sem, q_sem, key_sem = refs[24:]
    layer = lax.axis_index("depth")
    row_at = lax.axis_index("row")
    col_at = lax.axis_index("col")
    core = row_at & 1
    z = col_at & 7
    y_hi = col_at >> 3
    y = y_hi * 4 + (row_at >> 1)
    for d in range(8):
        origin = (z - d) & 7
        slot = (origin >> 2) * 2 + (origin & 1)

        @pl.when(((origin >> 1) & 1) == core)
        def _():
            pltpu.make_async_copy(x_refs[d], x_buf.at[slot], x_sem.at[slot]).start()

        source = (y - d) & 7
        place = (source >> 2) * 2 + (source & 1)

        @pl.when(((source >> 1) & 1) == y_hi)
        def _():
            pltpu.make_async_copy(qa_refs[d], q_buf.at[place, 0], q_sem.at[place, 0]).start()
            pltpu.make_async_copy(qb_refs[d], q_buf.at[place, 1], q_sem.at[place, 1]).start()

    keep_ref[...] = jnp.zeros_like(keep_ref)
    send_ref[...] = jnp.zeros_like(send_ref)
    for slot in range(4):
        pltpu.make_async_copy(x_refs[0], x_buf.at[slot], x_sem.at[slot]).wait()
        for half in range(2):
            pltpu.make_async_copy(qa_refs[0], q_buf.at[slot, half], q_sem.at[slot, half]).wait()

    lane = lax.broadcasted_iota(jnp.int32, (META, 128), 1)
    packed = jnp.zeros((META, 128), jnp.float32)
    for slot in range(4):
        for half in range(2):
            at = half * MSG + 2 * TILE
            x_rows = x_buf[slot, at : at + META, :128].astype(jnp.float32)
            q_rows = q_buf[slot, half, 2 * TILE :, :128].astype(jnp.float32)
            packed = jnp.where(lane == slot * 2 + half, x_rows, packed)
            packed = jnp.where(lane == 8 + slot * 2 + half, q_rows, packed)
    key_vec[...] = packed[:8].astype(jnp.int32)
    fetch = pltpu.make_async_copy(key_vec, keys, key_sem)
    fetch.start()
    fetch.wait()

    for h, out_ref in enumerate((keep_ref, send_ref)):

        def tile_step(i, carry, h=h, out_ref=out_ref):
            slot = i >> 1
            s = i & 1
            k4 = slot >> 1
            k2 = slot & 1
            key = keys[s, slot * 2 + h]
            inner = k2 * 4 + key
            start = pl.multiple_of(h * MSG + s * TILE, 16)
            for b in range(2):
                place = b * 2 + k4
                match = jnp.int32(-1)
                for j in range(4):
                    match = jnp.where(keys[j & 1, 8 + place * 2 + (j >> 1)] == inner, j, match)

                @pl.when((key >= 0) & (match >= 0))
                def _():
                    q_start = pl.multiple_of((match & 1) * TILE, 16)
                    out_ref[b] += jnp.dot(
                        x_buf[slot, pl.ds(start, TILE), :],
                        q_buf[place, match >> 1, pl.ds(q_start, TILE), :],
                        preferred_element_type=jnp.float32,
                    )

            @pl.when((key >= 0) & (layer == 0) & (y_hi == 0) & (k4 == 0) & (inner == z))
            def _():
                out_ref[core] -= 3.0 * x_buf[slot, pl.ds(start, TILE), :].astype(jnp.float32)

            return carry

        lax.fori_loop(0, 8, tile_step, 0)


def products(x_pieces, qa_pieces, qb_pieces):
    block = jax.ShapeDtypeStruct((2, TILE, TILE), jnp.float32)
    return pl.pallas_call(
        product_kernel,
        out_shape=(block, block),
        in_specs=[pl.BlockSpec(memory_space=pltpu.HBM)] * 24,
        out_specs=(pl.BlockSpec(memory_space=pltpu.VMEM),) * 2,
        scratch_shapes=[
            pltpu.VMEM((4, 2 * MSG, TILE), jnp.bfloat16),
            pltpu.VMEM((4, 2, MSG, TILE), jnp.bfloat16),
            pltpu.VMEM((8, 128), jnp.int32),
            pltpu.SMEM((8, 128), jnp.int32),
            pltpu.SemaphoreType.DMA((4,)),
            pltpu.SemaphoreType.DMA((4, 2)),
            pltpu.SemaphoreType.DMA,
        ],
        compiler_params=pltpu.CompilerParams(vmem_limit_bytes=24 * 1024 * 1024),
        cost_estimate=pl.CostEstimate(flops=2**28, bytes_accessed=5 * 2**20, transcendentals=0),
    )(*x_pieces, *qa_pieces, *qb_pieces)


def on_device(matrix_tiles, matrix_where, matrix_count, square_tiles, square_where, square_count):
    layer_at = lax.axis_index("depth")
    row_at = lax.axis_index("row")
    col_at = lax.axis_index("col")
    x_live = jnp.arange(2, dtype=jnp.int32) < matrix_count[0]
    q_live = jnp.arange(4, dtype=jnp.int32) < square_count[0]
    x_key = jnp.where(x_live, matrix_where[:, 1] - layer_at * KDEP - col_at * XSLAB, -1)
    q_key = jnp.where(q_live, square_where[:, 0] - layer_at * KDEP - row_at * QSLAB, -1)

    permute = functools.partial(lax.ppermute, axis_name=ROW_COL)
    with jax.named_scope("pack_matrix"):
        own_x = with_keys(matrix_tiles, x_key)
    with jax.named_scope("pair_matrix"):
        other_x = permute(own_x, perm=core_pairs())
        x_message = jnp.concatenate([own_x, other_x], axis=0)
    with jax.named_scope("pack_square"):
        qa = with_keys(square_tiles[:2], q_key[:2])
        qb = with_keys(square_tiles[2:], q_key[2:])

    x_pieces = [x_message] + [None] * 7
    qa_pieces = [qa] + [None] * 7
    qb_pieces = [qb] + [None] * 7
    right = [qa, qb, x_message]
    left = [qa, qb, x_message]
    for step in range(1, 5):
        with jax.named_scope("ring"):
            right[0] = permute(right[0], perm=y_pairs(step, 1, 4))
            qa_pieces[step] = right[0]
            if step < 4:
                left[0] = permute(left[0], perm=y_pairs(step, -1, 3))
                qa_pieces[8 - step] = left[0]
                right[1] = permute(right[1], perm=y_pairs(step, 1, 3))
                qb_pieces[step] = right[1]
            left[1] = permute(left[1], perm=y_pairs(step, -1, 4))
            qb_pieces[8 - step] = left[1]
            right[2] = permute(right[2], perm=z_pairs(step, 1))
            x_pieces[step] = right[2]
            if step < 4:
                left[2] = permute(left[2], perm=z_pairs(step, -1))
                x_pieces[8 - step] = left[2]

    keep, send = products(x_pieces, qa_pieces, qb_pieces)
    with jax.named_scope("pair_sum"):
        part = keep + permute(send, perm=swap_pairs())
    with jax.named_scope("scatter_sum"):
        groups = [
            [layer * 16 + y_hi * 8 + z for y_hi in range(2) for layer in range(8)] for z in range(8)
        ]
        shares = lax.all_to_all(
            part.reshape(16, TILE // 8, TILE), ("depth", "col"), 0, 0, axis_index_groups=groups
        )
        own = -0.5 * jnp.sum(shares, axis=0)
    with jax.named_scope("gather_rows"):
        spread = jnp.broadcast_to(own[None], (8, TILE // 8, TILE))
        return lax.all_to_all(spread, "depth", 0, 0).reshape(TILE, TILE)


def solution(mesh):
    in_specs = (
        P(("depth", "row", "col"), None, None),
        P(("depth", "row", "col"), None),
        P(("depth", "row", "col")),
        P(("depth", "row", "col"), None, None),
        P(("depth", "row", "col"), None),
        P(("depth", "row", "col")),
    )
    return jax.shard_map(
        on_device, mesh=mesh, in_specs=in_specs, out_specs=P("row", "col"), check_vma=False
    )
```

time: 421 us -> 142 us (0.34)
  waiting for transfers between devices: 382 us -> 14.7 us
  starting transfers between devices: 0.09 us -> 71.1 us
  blocking collectives: 0 us -> 48 us
  matrix products: 18.8 us -> 0 us
  between operations: 14.5 us -> 1.74 us
    all_gather x2 -> x0, waiting for transfers between devices: 299 us -> none  [the longest x1 213 us: on_device(): shard_piece = lax.all_gather(matrix_own, 'col', axis=0, tiled=True)]
    psum x1 -> x0, waiting for transfers between devices: 82.8 us -> none  [on_device(): return lax.psum(layer_part, 'depth')]
    ppermute x0 -> x23, starting transfers between devices: none -> 71.1 us  [the longest x3 14.9 us: on_device(): left[2] = permute(left[2], perm=z_pairs(step, -1))]
    all_to_all x0 -> x2, blocking collectives: none -> 48 us  [the longest x1 33.1 us: on_device(): lax.all_to_all(part.reshape(16, TILE // 8, TILE), ('depth', 'col'), 0, 0,...]
    dot_general x4 -> x0, matrix products: 18.8 us -> none  [the longest x1 8.8 us: block_update(): jnp.einsum('nab,nbc->ac', piece_tiles, square_rows, preferred_element_typ...]
    ppermute x0 -> x23, waiting for transfers between devices: none -> 14.7 us  [the longest x4 6.63 us: on_device(): left[1] = permute(left[1], perm=y_pairs(step, -1, 4))]
  transfers between devices with their start and end apart: 3 -> 23, of which waited for: 3 -> 9; matrix products, arithmetic and copies ran while one was open for 2% -> 0% of each run, Pallas kernels for 0% -> 0%
where the time goes in v1:
time: 142 us
  starting transfers between devices  71.1 us (50%)
  blocking collectives  48 us (34%)
  waiting for transfers between devices  14.7 us (10%)
  Pallas kernels  2.75 us (2%)
  other arithmetic  2.3 us (2%)
  between operations  1.74 us (1%)
    all_to_all x1, blocking collectives, on_device(): lax.all_to_all(part.reshape(16, TILE // 8, TILE), ('depth', 'col'), 0, 0,...  33.1 us
    all_to_all x1, blocking collectives, on_device(): return lax.all_to_all(spread, 'depth', 0, 0).reshape(TILE, TILE)  14.9 us
    ppermute x3, starting transfers between devices, on_device(): left[2] = permute(left[2], perm=z_pairs(step, -1))  14.9 us
    ppermute x4, starting transfers between devices, on_device(): left[1] = permute(left[1], perm=y_pairs(step, -1, 4))  14.1 us
    ppermute x4, starting transfers between devices, on_device(): right[0] = permute(right[0], perm=y_pairs(step, 1, 4))  9.48 us
    ppermute x4, starting transfers between devices, on_device(): right[2] = permute(right[2], perm=z_pairs(step, 1))  9.13 us
    ppermute x3, starting transfers between devices, on_device(): left[0] = permute(left[0], perm=y_pairs(step, -1, 3))  8.99 us
    ppermute x1, starting transfers between devices, on_device(): part = keep + permute(send, perm=swap_pairs())  6.73 us
  transfers between devices with their start and end apart: 23, of which 9 were waited for; matrix products, arithmetic and copies ran while one was open for 0% of the time, Pallas kernels for 0%

profile of v1, /device:TPU:2, one launch (start us, length us, event | category | flops | bytes accessed | tf_op | source)
XLA Modules:
  0.0 141.5 jit_solution(18344795350390756322)
XLA Ops:
  0.0 0.0 copy-start
  0.0 0.0 copy-start.2
  0.7 0.9 subtract_reduce_fusion
  1.6 0.1 broadcast_in_dim.17
  1.7 1.0 pad_maximum_fusion.1
  2.6 1.3 collective-permute-start
  4.6 0.0 copy-done.2
  4.6 0.0 copy-start.1
  4.6 1.5 %collective-permute-done = bf16[528,256]{1,0:T(8,128)(2,1)S(1)} collective-permute-done((bf16[528,256]{1,0:T(8,128)(2,1)S(1)}, bf16[528,256]{1,0:T(8,128)(2,1)S(1)}, u32[]{:S(2)}, u32[]{:S(2)}) %collective-permute-start) | collective-permute-done | bytes 270368 | tf_op jit(solution)/shard_map/pair_matrix/ppermute | solution.py:176
  6.1 0.0 copy-done
  6.1 5.2 %collective-permute-start.1 = (bf16[1056,256]{1,0:T(8,128)(2,1)S(1)}, bf16[1056,256]{1,0:T(8,128)(2,1)S(1)}, u32[]{:S(2)}, u32[]{:S(2)}) collective-permute-start(bf16[1056,256]{1,0:T(8,128)(2,1)S(1)} %pad_maximum_fusion.refs_0_), channel_id=1, source_target_pairs={{0,1},{1,2},{4,5},{5,6},{18,19},{19,20},{22,23},{23,16},{32,33},{3... | collective-permute-start | bytes 1622024 | tf_op jit(solution)/shard_map/ring/ppermute | solution.py:198
  11.4 0.1 fusion.5
  11.4 0.0 copy-done.1
  11.5 12.3 %collective-permute-start.5 = (bf16[1056,256]{1,0:T(8,128)(2,1)S(1)}, bf16[1056,256]{1,0:T(8,128)(2,1)S(1)}, u32[]{:S(2)}, u32[]{:S(2)}) collective-permute-start(bf16[1056,256]{1,0:T(8,128)(2,1)S(1)} %pad_maximum_fusion.refs_0_), channel_id=1, source_target_pairs={{0,7},{1,0},{4,3},{5,4},{18,17},{19,18},{22,21},{23,22},{32,39},{3... | collective-permute-start | bytes 1622024 | tf_op jit(solution)/shard_map/ring/ppermute | solution.py:201
  23.7 0.0 collective-permute-done.1.refs_1_
  23.8 0.7 collective-permute-start.2
  24.5 0.1 pad_maximum_fusion.3.refs_16_
  24.6 1.3 collective-permute-start.18
  25.9 4.6 %collective-permute-start.15 = (bf16[528,256]{1,0:T(8,128)(2,1)S(1)}, bf16[528,256]{1,0:T(8,128)(2,1)S(1)}, u32[]{:S(2)}, u32[]{:S(2)}) collective-permute-start(bf16[528,256]{1,0:T(8,128)(2,1)S(1)} %pad_maximum_fusion.3.refs_16_), channel_id=1, source_target_pairs={{0,32},{1,33},{2,34},{3,35},{4,36},{5,37},{6,38},{7,39},{16,48},{1... | collective-permute-start | bytes 811016 | tf_op jit(solution)/shard_map/ring/ppermute | solution.py:194
  30.5 0.1 pad_maximum_fusion.2.refs_8_
  30.6 1.3 collective-permute-start.12
  31.9 1.0 collective-permute-done.18.refs_23_
  33.0 3.6 %collective-permute-start.8 = (bf16[528,256]{1,0:T(8,128)(2,1)S(1)}, bf16[528,256]{1,0:T(8,128)(2,1)S(1)}, u32[]{:S(2)}, u32[]{:S(2)}) collective-permute-start(bf16[528,256]{1,0:T(8,128)(2,1)S(1)} %pad_maximum_fusion.2.refs_8_), channel_id=1, source_target_pairs={{0,32},{1,33},{2,34},{3,35},{4,36},{5,37},{6,38},{7,39},{16,48},{1... | collective-permute-start | bytes 811016 | tf_op jit(solution)/shard_map/ring/ppermute | solution.py:189
  36.6 0.0 collective-permute-done.15.refs_17_
  36.6 1.3 collective-permute-start.19
  37.9 0.0 collective-permute-done.5.refs_7_
  37.9 1.9 %collective-permute-start.6 = (bf16[1056,256]{1,0:T(8,128)(2,1)S(1)}, bf16[1056,256]{1,0:T(8,128)(2,1)S(1)}, u32[]{:S(2)}, u32[]{:S(2)}) collective-permute-start(bf16[1056,256]{1,0:T(8,128)(2,1)S(1)} %collective-permute-done.5.refs_7_), channel_id=1, source_target_pairs={{0,7},{3,2},{4,3},{7,6},{17,16},{18,17},{21,20},{22,21},{32,39},{3... | collective-permute-start | bytes 1622024 | tf_op jit(solution)/shard_map/ring/ppermute | solution.py:201
  39.8 0.0 collective-permute-done.2.refs_2_
  39.8 1.3 collective-permute-start.3
  41.1 0.6 collective-permute-done.12.refs_15_
  41.7 0.7 collective-permute-start.16
  42.4 0.9 collective-permute-done.8.refs_9_
  43.3 1.3 collective-permute-start.13
  44.6 3.1 %collective-permute-done.19.refs_22_ = bf16[528,256]{1,0:T(8,128)(2,1)S(1)} collective-permute-done((bf16[528,256]{1,0:T(8,128)(2,1)S(1)}, bf16[528,256]{1,0:T(8,128)(2,1)S(1)}, u32[]{:S(2)}, u32[]{:S(2)}) %collective-permute-start.19) | collective-permute-done | bytes 270368 | tf_op jit(solution)/shard_map/ring/ppermute | solution.py:196
  47.7 0.7 collective-permute-start.9
  48.4 0.0 collective-permute-done.16.refs_18_
  48.4 9.6 %collective-permute-start.20 = (bf16[528,256]{1,0:T(8,128)(2,1)S(1)}, bf16[528,256]{1,0:T(8,128)(2,1)S(1)}, u32[]{:S(2)}, u32[]{:S(2)}) collective-permute-start(bf16[528,256]{1,0:T(8,128)(2,1)S(1)} %collective-permute-done.19.refs_22_), channel_id=1, source_target_pairs={{0,104},{1,105},{2,106},{3,107},{4,108},{5,109},{6,110},{7,111},{1... | collective-permute-start | bytes 811016 | tf_op jit(solution)/shard_map/ring/ppermute | solution.py:196
  57.9 0.0 collective-permute-done.13.refs_14_
  58.0 1.3 collective-permute-start.17
  59.3 0.0 collective-permute-done.9.refs_10_
  59.3 1.3 collective-permute-start.10
  60.6 0.0 collective-permute-done.6.refs_6_
  60.6 0.7 collective-permute-start.7
  61.3 0.0 collective-permute-done.3.refs_3_
  61.3 1.9 %collective-permute-start.4 = (bf16[1056,256]{1,0:T(8,128)(2,1)S(1)}, bf16[1056,256]{1,0:T(8,128)(2,1)S(1)}, u32[]{:S(2)}, u32[]{:S(2)}) collective-permute-start(bf16[1056,256]{1,0:T(8,128)(2,1)S(1)} %collective-permute-done.3.refs_3_), channel_id=1, source_target_pairs={{0,1},{3,4},{4,5},{7,0},{17,18},{18,19},{21,22},{22,23},{32,33},{3... | collective-permute-start | bytes 1622024 | tf_op jit(solution)/shard_map/ring/ppermute | solution.py:198
  63.2 0.0 collective-permute-done.20.refs_21_
  63.2 6.4 %collective-permute-start.14 = (bf16[528,256]{1,0:T(8,128)(2,1)S(1)}, bf16[528,256]{1,0:T(8,128)(2,1)S(1)}, u32[]{:S(2)}, u32[]{:S(2)}) collective-permute-start(bf16[528,256]{1,0:T(8,128)(2,1)S(1)} %collective-permute-done.13.refs_14_), channel_id=1, source_target_pairs={{0,104},{1,105},{2,106},{3,107},{4,108},{5,109},{6,110},{7,111},{1... | collective-permute-start | bytes 811016 | tf_op jit(solution)/shard_map/ring/ppermute | solution.py:192
  69.6 0.0 collective-permute-done.17.refs_19_
  69.7 1.9 %collective-permute-start.21 = (bf16[528,256]{1,0:T(8,128)(2,1)S(1)}, bf16[528,256]{1,0:T(8,128)(2,1)S(1)}, u32[]{:S(2)}, u32[]{:S(2)}) collective-permute-start(bf16[528,256]{1,0:T(8,128)(2,1)S(1)} %collective-permute-done.20.refs_21_), channel_id=1, source_target_pairs={{0,104},{1,105},{2,106},{3,107},{4,108},{5,109},{6,110},{7,111},{1... | collective-permute-start | bytes 811016 | tf_op jit(solution)/shard_map/ring/ppermute | solution.py:196
  71.6 0.0 collective-permute-done.10.refs_11_
  71.6 3.9 %collective-permute-start.11 = (bf16[528,256]{1,0:T(8,128)(2,1)S(1)}, bf16[528,256]{1,0:T(8,128)(2,1)S(1)}, u32[]{:S(2)}, u32[]{:S(2)}) collective-permute-start(bf16[528,256]{1,0:T(8,128)(2,1)S(1)} %collective-permute-done.10.refs_11_), channel_id=1, source_target_pairs={{0,32},{1,33},{2,34},{3,35},{4,36},{5,37},{6,38},{7,39},{16,48},{1... | collective-permute-start | bytes 811016 | tf_op jit(solution)/shard_map/ring/ppermute | solution.py:189
  75.5 0.0 collective-permute-done.14.refs_13_
  75.5 2.5 %collective-permute-done.21.refs_20_ = bf16[528,256]{1,0:T(8,128)(2,1)S(1)} collective-permute-done((bf16[528,256]{1,0:T(8,128)(2,1)S(1)}, bf16[528,256]{1,0:T(8,128)(2,1)S(1)}, u32[]{:S(2)}, u32[]{:S(2)}) %collective-permute-start.21) | collective-permute-done | bytes 270368 | tf_op jit(solution)/shard_map/ring/ppermute | solution.py:196
  78.0 3.3 %collective-permute-done.11.refs_12_ = bf16[528,256]{1,0:T(8,128)(2,1)S(1)} collective-permute-done((bf16[528,256]{1,0:T(8,128)(2,1)S(1)}, bf16[528,256]{1,0:T(8,128)(2,1)S(1)}, u32[]{:S(2)}, u32[]{:S(2)}) %collective-permute-start.11) | collective-permute-done | bytes 270368 | tf_op jit(solution)/shard_map/ring/ppermute | solution.py:189
  81.3 0.0 collective-permute-done.7.refs_5_
  81.3 0.3 collective-permute-done.4.refs_4_
  81.6 2.7 %shard_map.64 = (f32[2,256,256]{2,1,0:T(8,128)S(1)}, f32[2,256,256]{2,1,0:T(8,128)S(1)}) custom-call(bf16[1056,256]{1,0:T(8,128)(2,1)S(1)} %pad_maximum_fusion.refs_0_, bf16[1056,256]{1,0:T(8,128)(2,1)S(1)} %collective-permute-done.1.refs_1_, bf16[1056,256]{1,0:T(8,128)(2,1)S(1)} %collective-permute-done.2.refs_2_, ...), custom_call_target="tpu_custom_call" | custom-call | flops 268435456 | bytes 5242880 | tf_op jit(solution)/shard_map/pallas_call | solution.py:144
  84.4 6.7 %collective-permute-start.22 = (f32[2,256,256]{2,1,0:T(8,128)S(1)}, f32[2,256,256]{2,1,0:T(8,128)S(1)}, u32[]{:S(2)}, u32[]{:S(2)}) collective-permute-start(f32[2,256,256]{2,1,0:T(8,128)S(1)} %get-tuple-element.8), channel_id=1, source_target_pairs={{0,16},{1,17},{2,18},{3,19},{4,20},{5,21},{6,22},{7,23},{16,0},{17... | collective-permute-start | bytes 1572872 | tf_op jit(solution)/shard_map/pair_sum/ppermute | solution.py:206
  91.1 1.5 %collective-permute-done.22 = f32[2,256,256]{2,1,0:T(8,128)S(1)} collective-permute-done((f32[2,256,256]{2,1,0:T(8,128)S(1)}, f32[2,256,256]{2,1,0:T(8,128)S(1)}, u32[]{:S(2)}, u32[]{:S(2)}) %collective-permute-start.22) | collective-permute-done | bytes 524320 | tf_op jit(solution)/shard_map/pair_sum/ppermute | solution.py:206
  92.6 0.1 add.9
  92.7 33.1 %all_to_all.10 = f32[16,32,256]{2,1,0:T(8,128)S(1)} all-to-all(f32[16,32,256]{2,1,0:T(8,128)S(1)} %bitcast.11), channel_id=1, replica_groups={{0,128,256,384,512,640,768,896,8,136,264,392,520,648,776,904},{1,129,25..., dimensions={0} | all-to-all | bytes 1048576 | tf_op jit(solution)/shard_map/scatter_sum/all_to_all | solution.py:211
  125.9 14.9 %all_to_all.11 = f32[8,32,256]{2,1,0:T(8,128)S(1)} all-to-all(f32[8,32,256]{2,1,0:T(8,128)S(1)} %broadcast_in_dim.37), channel_id=1, replica_groups=mesh['depth'=8,'row'=8,'col'=16] {'depth'}, dimensions={0} | all-to-all | bytes 524288 | tf_op jit(solution)/shard_map/gather_rows/all_to_all | solution.py:217
  140.8 0.7 copy.10
  (10 shorter events, 0.2 us)
Async XLA Ops:
  0.0 6.1 %copy-start = (bf16[2,256,256]{2,1,0:T(8,128)(2,1)S(1)}, bf16[2,256,256]{2,1,0:T(8,128)(2,1)}, u32[]{:S(2)}) copy-start(bf16[2,256,256]{2,1,0:T(8,128)(2,1)} %param.6) | copy-start | bytes 786436
  0.0 4.6 %copy-start.2 = (s32[4,2]{0,1:T(2,128)S(1)}, s32[4,2]{0,1:T(2,128)}, u32[]{:S(2)}) copy-start(s32[4,2]{0,1:T(2,128)} %param.10) | copy-start | bytes 100
  2.6 3.4 %collective-permute-start = (bf16[528,256]{1,0:T(8,128)(2,1)S(1)}, bf16[528,256]{1,0:T(8,128)(2,1)S(1)}, u32[]{:S(2)}, u32[]{:S(2)}) collective-permute-start(bf16[528,256]{1,0:T(8,128)(2,1)S(1)} %pad_maximum_fusion.1), channel_id=1, source_target_pairs={{16,0},{17,1},{20,4},{21,5},{2,18},{3,19},{6,22},{7,23},{48,32},{4... | collective-permute-start | bytes 811016 | tf_op jit(solution)/shard_map/pair_matrix/ppermute | solution.py:176
  4.6 6.8 %copy-start.1 = (bf16[4,256,256]{2,1,0:T(8,128)(2,1)S(1)}, bf16[4,256,256]{2,1,0:T(8,128)(2,1)}, u32[]{:S(2)}) copy-start(bf16[4,256,256]{2,1,0:T(8,128)(2,1)} %param.9) | copy-start | bytes 1572868
  6.1 17.6 %collective-permute-start.1 = (bf16[1056,256]{1,0:T(8,128)(2,1)S(1)}, bf16[1056,256]{1,0:T(8,128)(2,1)S(1)}, u32[]{:S(2)}, u32[]{:S(2)}) collective-permute-start(bf16[1056,256]{1,0:T(8,128)(2,1)S(1)} %pad_maximum_fusion.refs_0_), channel_id=1, source_target_pairs={{0,1},{1,2},{4,5},{5,6},{18,19},{19,20},{22,23},{23,16},{32,33},{3... | collective-permute-start | bytes 1622024 | tf_op jit(solution)/shard_map/ring/ppermute | solution.py:198
  11.5 26.4 %collective-permute-start.5 = (bf16[1056,256]{1,0:T(8,128)(2,1)S(1)}, bf16[1056,256]{1,0:T(8,128)(2,1)S(1)}, u32[]{:S(2)}, u32[]{:S(2)}) collective-permute-start(bf16[1056,256]{1,0:T(8,128)(2,1)S(1)} %pad_maximum_fusion.refs_0_), channel_id=1, source_target_pairs={{0,7},{1,0},{4,3},{5,4},{18,17},{19,18},{22,21},{23,22},{32,39},{3... | collective-permute-start | bytes 1622024 | tf_op jit(solution)/shard_map/ring/ppermute | solution.py:201
  23.8 16.1 %collective-permute-start.2 = (bf16[1056,256]{1,0:T(8,128)(2,1)S(1)}, bf16[1056,256]{1,0:T(8,128)(2,1)S(1)}, u32[]{:S(2)}, u32[]{:S(2)}) collective-permute-start(bf16[1056,256]{1,0:T(8,128)(2,1)S(1)} %collective-permute-done.1.refs_1_), channel_id=1, source_target_pairs={{1,2},{2,3},{5,6},{6,7},{16,17},{19,20},{20,21},{23,16},{33,34},{3... | collective-permute-start | bytes 1622024 | tf_op jit(solution)/shard_map/ring/ppermute | solution.py:198
  24.6 8.4 %collective-permute-start.18 = (bf16[528,256]{1,0:T(8,128)(2,1)S(1)}, bf16[528,256]{1,0:T(8,128)(2,1)S(1)}, u32[]{:S(2)}, u32[]{:S(2)}) collective-permute-start(bf16[528,256]{1,0:T(8,128)(2,1)S(1)} %pad_maximum_fusion.3.refs_16_), channel_id=1, source_target_pairs={{32,0},{33,1},{34,2},{35,3},{36,4},{37,5},{38,6},{39,7},{48,16},{4... | collective-permute-start | bytes 811016 | tf_op jit(solution)/shard_map/ring/ppermute | solution.py:196
  25.9 10.7 %collective-permute-start.15 = (bf16[528,256]{1,0:T(8,128)(2,1)S(1)}, bf16[528,256]{1,0:T(8,128)(2,1)S(1)}, u32[]{:S(2)}, u32[]{:S(2)}) collective-permute-start(bf16[528,256]{1,0:T(8,128)(2,1)S(1)} %pad_maximum_fusion.3.refs_16_), channel_id=1, source_target_pairs={{0,32},{1,33},{2,34},{3,35},{4,36},{5,37},{6,38},{7,39},{16,48},{1... | collective-permute-start | bytes 811016 | tf_op jit(solution)/shard_map/ring/ppermute | solution.py:194
  30.6 11.1 %collective-permute-start.12 = (bf16[528,256]{1,0:T(8,128)(2,1)S(1)}, bf16[528,256]{1,0:T(8,128)(2,1)S(1)}, u32[]{:S(2)}, u32[]{:S(2)}) collective-permute-start(bf16[528,256]{1,0:T(8,128)(2,1)S(1)} %pad_maximum_fusion.2.refs_8_), channel_id=1, source_target_pairs={{32,0},{33,1},{34,2},{35,3},{36,4},{37,5},{38,6},{39,7},{48,16},{4... | collective-permute-start | bytes 811016 | tf_op jit(solution)/shard_map/ring/ppermute | solution.py:192
  33.0 10.3 %collective-permute-start.8 = (bf16[528,256]{1,0:T(8,128)(2,1)S(1)}, bf16[528,256]{1,0:T(8,128)(2,1)S(1)}, u32[]{:S(2)}, u32[]{:S(2)}) collective-permute-start(bf16[528,256]{1,0:T(8,128)(2,1)S(1)} %pad_maximum_fusion.2.refs_8_), channel_id=1, source_target_pairs={{0,32},{1,33},{2,34},{3,35},{4,36},{5,37},{6,38},{7,39},{16,48},{1... | collective-permute-start | bytes 811016 | tf_op jit(solution)/shard_map/ring/ppermute | solution.py:189
  36.6 11.1 %collective-permute-start.19 = (bf16[528,256]{1,0:T(8,128)(2,1)S(1)}, bf16[528,256]{1,0:T(8,128)(2,1)S(1)}, u32[]{:S(2)}, u32[]{:S(2)}) collective-permute-start(bf16[528,256]{1,0:T(8,128)(2,1)S(1)} %collective-permute-done.18.refs_23_), channel_id=1, source_target_pairs={{32,0},{33,1},{34,2},{35,3},{36,4},{37,5},{38,6},{39,7},{48,16},{4... | collective-permute-start | bytes 811016 | tf_op jit(solution)/shard_map/ring/ppermute | solution.py:196
  37.9 22.7 %collective-permute-start.6 = (bf16[1056,256]{1,0:T(8,128)(2,1)S(1)}, bf16[1056,256]{1,0:T(8,128)(2,1)S(1)}, u32[]{:S(2)}, u32[]{:S(2)}) collective-permute-start(bf16[1056,256]{1,0:T(8,128)(2,1)S(1)} %collective-permute-done.5.refs_7_), channel_id=1, source_target_pairs={{0,7},{3,2},{4,3},{7,6},{17,16},{18,17},{21,20},{22,21},{32,39},{3... | collective-permute-start | bytes 1622024 | tf_op jit(solution)/shard_map/ring/ppermute | solution.py:201
  39.8 21.5 %collective-permute-start.3 = (bf16[1056,256]{1,0:T(8,128)(2,1)S(1)}, bf16[1056,256]{1,0:T(8,128)(2,1)S(1)}, u32[]{:S(2)}, u32[]{:S(2)}) collective-permute-start(bf16[1056,256]{1,0:T(8,128)(2,1)S(1)} %collective-permute-done.2.refs_2_), channel_id=1, source_target_pairs={{2,3},{3,4},{6,7},{7,0},{16,17},{17,18},{20,21},{21,22},{34,35},{3... | collective-permute-start | bytes 1622024 | tf_op jit(solution)/shard_map/ring/ppermute | solution.py:198
  41.7 6.7 %collective-permute-start.16 = (bf16[528,256]{1,0:T(8,128)(2,1)S(1)}, bf16[528,256]{1,0:T(8,128)(2,1)S(1)}, u32[]{:S(2)}, u32[]{:S(2)}) collective-permute-start(bf16[528,256]{1,0:T(8,128)(2,1)S(1)} %collective-permute-done.15.refs_17_), channel_id=1, source_target_pairs={{32,64},{33,65},{34,66},{35,67},{36,68},{37,69},{38,70},{39,71},{4... | collective-permute-start | bytes 811016 | tf_op jit(solution)/shard_map/ring/ppermute | solution.py:194
  43.3 14.7 %collective-permute-start.13 = (bf16[528,256]{1,0:T(8,128)(2,1)S(1)}, bf16[528,256]{1,0:T(8,128)(2,1)S(1)}, u32[]{:S(2)}, u32[]{:S(2)}) collective-permute-start(bf16[528,256]{1,0:T(8,128)(2,1)S(1)} %collective-permute-done.12.refs_15_), channel_id=1, source_target_pairs={{32,0},{33,1},{34,2},{35,3},{36,4},{37,5},{38,6},{39,7},{48,16},{4... | collective-permute-start | bytes 811016 | tf_op jit(solution)/shard_map/ring/ppermute | solution.py:192
  47.7 11.6 %collective-permute-start.9 = (bf16[528,256]{1,0:T(8,128)(2,1)S(1)}, bf16[528,256]{1,0:T(8,128)(2,1)S(1)}, u32[]{:S(2)}, u32[]{:S(2)}) collective-permute-start(bf16[528,256]{1,0:T(8,128)(2,1)S(1)} %collective-permute-done.8.refs_9_), channel_id=1, source_target_pairs={{32,64},{33,65},{34,66},{35,67},{36,68},{37,69},{38,70},{39,71},{4... | collective-permute-start | bytes 811016 | tf_op jit(solution)/shard_map/ring/ppermute | solution.py:189
  48.4 14.9 %collective-permute-start.20 = (bf16[528,256]{1,0:T(8,128)(2,1)S(1)}, bf16[528,256]{1,0:T(8,128)(2,1)S(1)}, u32[]{:S(2)}, u32[]{:S(2)}) collective-permute-start(bf16[528,256]{1,0:T(8,128)(2,1)S(1)} %collective-permute-done.19.refs_22_), channel_id=1, source_target_pairs={{0,104},{1,105},{2,106},{3,107},{4,108},{5,109},{6,110},{7,111},{1... | collective-permute-start | bytes 811016 | tf_op jit(solution)/shard_map/ring/ppermute | solution.py:196
  58.0 11.7 %collective-permute-start.17 = (bf16[528,256]{1,0:T(8,128)(2,1)S(1)}, bf16[528,256]{1,0:T(8,128)(2,1)S(1)}, u32[]{:S(2)}, u32[]{:S(2)}) collective-permute-start(bf16[528,256]{1,0:T(8,128)(2,1)S(1)} %collective-permute-done.16.refs_18_), channel_id=1, source_target_pairs={{64,96},{65,97},{66,98},{67,99},{68,100},{69,101},{70,102},{71,103... | collective-permute-start | bytes 811016 | tf_op jit(solution)/shard_map/ring/ppermute | solution.py:194
  59.3 12.3 %collective-permute-start.10 = (bf16[528,256]{1,0:T(8,128)(2,1)S(1)}, bf16[528,256]{1,0:T(8,128)(2,1)S(1)}, u32[]{:S(2)}, u32[]{:S(2)}) collective-permute-start(bf16[528,256]{1,0:T(8,128)(2,1)S(1)} %collective-permute-done.9.refs_10_), channel_id=1, source_target_pairs={{64,96},{65,97},{66,98},{67,99},{68,100},{69,101},{70,102},{71,103... | collective-permute-start | bytes 811016 | tf_op jit(solution)/shard_map/ring/ppermute | solution.py:189
  60.6 20.7 %collective-permute-start.7 = (bf16[1056,256]{1,0:T(8,128)(2,1)S(1)}, bf16[1056,256]{1,0:T(8,128)(2,1)S(1)}, u32[]{:S(2)}, u32[]{:S(2)}) collective-permute-start(bf16[1056,256]{1,0:T(8,128)(2,1)S(1)} %collective-permute-done.6.refs_6_), channel_id=1, source_target_pairs={{2,1},{3,2},{6,5},{7,6},{16,23},{17,16},{20,19},{21,20},{34,33},{3... | collective-permute-start | bytes 1622024 | tf_op jit(solution)/shard_map/ring/ppermute | solution.py:201
  61.3 20.3 %collective-permute-start.4 = (bf16[1056,256]{1,0:T(8,128)(2,1)S(1)}, bf16[1056,256]{1,0:T(8,128)(2,1)S(1)}, u32[]{:S(2)}, u32[]{:S(2)}) collective-permute-start(bf16[1056,256]{1,0:T(8,128)(2,1)S(1)} %collective-permute-done.3.refs_3_), channel_id=1, source_target_pairs={{0,1},{3,4},{4,5},{7,0},{17,18},{18,19},{21,22},{22,23},{32,33},{3... | collective-permute-start | bytes 1622024 | tf_op jit(solution)/shard_map/ring/ppermute | solution.py:198
  63.2 12.3 %collective-permute-start.14 = (bf16[528,256]{1,0:T(8,128)(2,1)S(1)}, bf16[528,256]{1,0:T(8,128)(2,1)S(1)}, u32[]{:S(2)}, u32[]{:S(2)}) collective-permute-start(bf16[528,256]{1,0:T(8,128)(2,1)S(1)} %collective-permute-done.13.refs_14_), channel_id=1, source_target_pairs={{0,104},{1,105},{2,106},{3,107},{4,108},{5,109},{6,110},{7,111},{1... | collective-permute-start | bytes 811016 | tf_op jit(solution)/shard_map/ring/ppermute | solution.py:192
  69.7 8.4 %collective-permute-start.21 = (bf16[528,256]{1,0:T(8,128)(2,1)S(1)}, bf16[528,256]{1,0:T(8,128)(2,1)S(1)}, u32[]{:S(2)}, u32[]{:S(2)}) collective-permute-start(bf16[528,256]{1,0:T(8,128)(2,1)S(1)} %collective-permute-done.20.refs_21_), channel_id=1, source_target_pairs={{0,104},{1,105},{2,106},{3,107},{4,108},{5,109},{6,110},{7,111},{1... | collective-permute-start | bytes 811016 | tf_op jit(solution)/shard_map/ring/ppermute | solution.py:196
  71.6 9.7 %collective-permute-start.11 = (bf16[528,256]{1,0:T(8,128)(2,1)S(1)}, bf16[528,256]{1,0:T(8,128)(2,1)S(1)}, u32[]{:S(2)}, u32[]{:S(2)}) collective-permute-start(bf16[528,256]{1,0:T(8,128)(2,1)S(1)} %collective-permute-done.10.refs_11_), channel_id=1, source_target_pairs={{0,32},{1,33},{2,34},{3,35},{4,36},{5,37},{6,38},{7,39},{16,48},{1... | collective-permute-start | bytes 811016 | tf_op jit(solution)/shard_map/ring/ppermute | solution.py:189
  84.4 8.3 %collective-permute-start.22 = (f32[2,256,256]{2,1,0:T(8,128)S(1)}, f32[2,256,256]{2,1,0:T(8,128)S(1)}, u32[]{:S(2)}, u32[]{:S(2)}) collective-permute-start(f32[2,256,256]{2,1,0:T(8,128)S(1)} %get-tuple-element.8), channel_id=1, source_target_pairs={{0,16},{1,17},{2,18},{3,19},{4,20},{5,21},{6,22},{7,23},{16,0},{17... | collective-permute-start | bytes 1572872 | tf_op jit(solution)/shard_map/pair_sum/ppermute | solution.py:206

commit v2 on v1

v2 whole, which is shorter than its diff:
```python
import functools

import jax
import jax.numpy as jnp
from jax import lax
from jax.experimental import pallas as pl
from jax.experimental.pallas import tpu as pltpu
from jax.sharding import PartitionSpec as P

TILE = 256
META = 16
X_ROWS = 2 * TILE + META
Q_ROWS = 4 * TILE + META
KDEP = 64
XSLAB = 4
QSLAB = 8
ROW_COL = ("row", "col")


def flat(y, core, z):
    return ((y & 3) * 2 + core) * 16 + (y >> 2) * 8 + z


def places():
    return [(y, core, z) for y in range(8) for core in range(2) for z in range(8)]


def swap_pairs():
    return [(flat(y, core, z), flat(y, 1 - core, z)) for y, core, z in places()]


def z_pairs(step, way):
    pairs = []
    for y, core, z in places():
        origin = (z - way * (step - 1)) % 8
        if (origin >> 1 & 1) == core:
            pairs.append((flat(y, core, z), flat(y, core, (z + way) % 8)))
    return pairs


def needed(origin, target):
    return (origin >> 1 & 1) == (target >> 2)


def y_pairs(step, reach):
    pairs = []
    for y, core, z in places():
        way = 1 - 2 * core
        origin = (y - way * (step - 1)) % 8
        if any(needed(origin, (origin + way * t) % 8) for t in range(step, reach + 1)):
            pairs.append((flat(y, core, z), flat((y + way) % 8, core, z)))
    return pairs


def share_pairs(step):
    return [
        (flat(y, core, z), flat(y, 1 - core, z))
        for y, core, z in places()
        if needed((y - (1 - 2 * core) * step) % 8, y)
    ]


def with_keys(tiles, keys):
    count = tiles.shape[0]
    rows = jnp.pad(keys, (0, META - count), constant_values=-1)
    rows = jnp.broadcast_to(rows[:, None], (META, TILE)).astype(jnp.bfloat16)
    return jnp.concatenate([tiles.reshape(count * TILE, TILE), rows], axis=0)


def product_kernel(*refs):
    x_refs, q_refs = refs[:8], refs[8:16]
    keep_ref, send_ref, x_buf, q_buf, key_vec, keys, x_sem, q_sem, key_sem = refs[16:]
    layer = lax.axis_index("depth")
    row_at = lax.axis_index("row")
    col_at = lax.axis_index("col")
    core = row_at & 1
    z = col_at & 7
    y_hi = col_at >> 3
    y = y_hi * 4 + (row_at >> 1)
    for d in range(8):
        origin = (z - d) & 7
        slot = (origin >> 2) * 2 + (origin & 1)

        @pl.when(((origin >> 1) & 1) == core)
        def _():
            pltpu.make_async_copy(x_refs[d], x_buf.at[slot], x_sem.at[slot]).start()

        source = (y - (1 - 2 * core) * (d if d < 5 else 4 - d)) & 7
        place = (source >> 2) * 2 + (source & 1)

        @pl.when(((source >> 1) & 1) == y_hi)
        def _():
            pltpu.make_async_copy(q_refs[d], q_buf.at[place], q_sem.at[place]).start()

    keep_ref[...] = jnp.zeros_like(keep_ref)
    send_ref[...] = jnp.zeros_like(send_ref)
    for slot in range(4):
        pltpu.make_async_copy(x_refs[0], x_buf.at[slot], x_sem.at[slot]).wait()
        pltpu.make_async_copy(q_refs[0], q_buf.at[slot], q_sem.at[slot]).wait()

    lane = lax.broadcasted_iota(jnp.int32, (META, 128), 1)
    packed = jnp.zeros((META, 128), jnp.float32)
    for slot in range(4):
        for half in range(2):
            at = half * X_ROWS + 2 * TILE
            x_rows = x_buf[slot, at : at + META, :128].astype(jnp.float32)
            packed = jnp.where(lane == slot * 2 + half, x_rows, packed)
        q_rows = q_buf[slot, 4 * TILE :, :128].astype(jnp.float32)
        packed = jnp.where(lane == 8 + slot, q_rows, packed)
    key_vec[...] = packed[:8].astype(jnp.int32)
    fetch = pltpu.make_async_copy(key_vec, keys, key_sem)
    fetch.start()
    fetch.wait()

    for h, out_ref in enumerate((keep_ref, send_ref)):

        def tile_step(i, carry, h=h, out_ref=out_ref):
            slot = i >> 1
            s = i & 1
            k4 = slot >> 1
            k2 = slot & 1
            key = keys[s, slot * 2 + h]
            inner = k2 * 4 + key
            start = pl.multiple_of(h * X_ROWS + s * TILE, 16)
            for b in range(2):
                place = b * 2 + k4
                match = jnp.int32(-1)
                for j in range(4):
                    match = jnp.where(keys[j, 8 + place] == inner, j, match)

                @pl.when((key >= 0) & (match >= 0))
                def _():
                    q_start = pl.multiple_of(match * TILE, 16)
                    out_ref[b] += jnp.dot(
                        x_buf[slot, pl.ds(start, TILE), :],
                        q_buf[place, pl.ds(q_start, TILE), :],
                        preferred_element_type=jnp.float32,
                    )

            @pl.when((key >= 0) & (layer == 0) & (y_hi == 0) & (k4 == 0) & (inner == z))
            def _():
                out_ref[core] -= 3.0 * x_buf[slot, pl.ds(start, TILE), :].astype(jnp.float32)

            return carry

        lax.fori_loop(0, 8, tile_step, 0)


def products(x_pieces, q_pieces):
    block = jax.ShapeDtypeStruct((2, TILE, TILE), jnp.float32)
    return pl.pallas_call(
        product_kernel,
        out_shape=(block, block),
        in_specs=[pl.BlockSpec(memory_space=pltpu.HBM)] * 16,
        out_specs=(pl.BlockSpec(memory_space=pltpu.VMEM),) * 2,
        scratch_shapes=[
            pltpu.VMEM((4, 2 * X_ROWS, TILE), jnp.bfloat16),
            pltpu.VMEM((4, Q_ROWS, TILE), jnp.bfloat16),
            pltpu.VMEM((8, 128), jnp.int32),
            pltpu.SMEM((8, 128), jnp.int32),
            pltpu.SemaphoreType.DMA((4,)),
            pltpu.SemaphoreType.DMA((4,)),
            pltpu.SemaphoreType.DMA,
        ],
        compiler_params=pltpu.CompilerParams(vmem_limit_bytes=24 * 1024 * 1024),
        cost_estimate=pl.CostEstimate(flops=2**28, bytes_accessed=5 * 2**20, transcendentals=0),
    )(*x_pieces, *q_pieces)


def on_device(matrix_tiles, matrix_where, matrix_count, square_tiles, square_where, square_count):
    layer_at = lax.axis_index("depth")
    row_at = lax.axis_index("row")
    col_at = lax.axis_index("col")
    x_live = jnp.arange(2, dtype=jnp.int32) < matrix_count[0]
    q_live = jnp.arange(4, dtype=jnp.int32) < square_count[0]
    x_key = jnp.where(x_live, matrix_where[:, 1] - layer_at * KDEP - col_at * XSLAB, -1)
    q_key = jnp.where(q_live, square_where[:, 0] - layer_at * KDEP - row_at * QSLAB, -1)

    permute = functools.partial(lax.ppermute, axis_name=ROW_COL)
    with jax.named_scope("pack"):
        own_q = with_keys(square_tiles, q_key)
        own_x = with_keys(matrix_tiles, x_key)
        both = jnp.concatenate([own_q, own_x], axis=0)
    with jax.named_scope("pair"):
        other = permute(both, perm=swap_pairs())
        other_q = other[:Q_ROWS]
        x_message = jnp.concatenate([own_x, other[Q_ROWS:]], axis=0)

    x_pieces = [x_message] + [None] * 7
    first = [own_q]
    shared = []
    second = other_q
    right = left = x_message
    for step in range(1, 5):
        with jax.named_scope("ring_square"):
            first.append(permute(first[-1], perm=y_pairs(step, 4)))
            if step < 4:
                second = permute(second, perm=y_pairs(step, 3))
                shared.append(permute(second, perm=share_pairs(step)))
        with jax.named_scope("ring_matrix"):
            right = permute(right, perm=z_pairs(step, 1))
            x_pieces[step] = right
            if step < 4:
                left = permute(left, perm=z_pairs(step, -1))
                x_pieces[8 - step] = left

    keep, send = products(x_pieces, first + shared)
    with jax.named_scope("pair_sum"):
        part = keep + permute(send, perm=swap_pairs())
    with jax.named_scope("scatter_sum"):
        groups = [
            [layer * 16 + y_hi * 8 + z for y_hi in range(2) for layer in range(8)] for z in range(8)
        ]
        shares = lax.all_to_all(
            part.reshape(16, TILE // 8, TILE), ("depth", "col"), 0, 0, axis_index_groups=groups
        )
        own = -0.5 * jnp.sum(shares, axis=0)
    with jax.named_scope("gather_rows"):
        spread = jnp.broadcast_to(own[None], (8, TILE // 8, TILE))
        return lax.all_to_all(spread, "depth", 0, 0).reshape(TILE, TILE)


def solution(mesh):
    in_specs = (
        P(("depth", "row", "col"), None, None),
        P(("depth", "row", "col"), None),
        P(("depth", "row", "col")),
        P(("depth", "row", "col"), None, None),
        P(("depth", "row", "col"), None),
        P(("depth", "row", "col")),
    )
    return jax.shard_map(
        on_device, mesh=mesh, in_specs=in_specs, out_specs=P("row", "col"), check_vma=False
    )
```

time: 142 us -> 127 us (0.89)
  starting transfers between devices: 71.1 us -> 51.1 us
  waiting for transfers between devices: 14.7 us -> 21.4 us
  blocking collectives: 48 us -> 45.6 us
    ppermute x22 -> x18, starting transfers between devices: 64.3 us -> 49.1 us  [the longest x3 19.1 us: on_device(): left = permute(left, perm=z_pairs(step, -1))]
    ppermute x22 -> x18, waiting for transfers between devices: 13.2 us -> 19.5 us  [the longest x3 6.31 us: on_device(): left = permute(left, perm=z_pairs(step, -1))]
    ppermute x1, starting transfers between devices: 6.73 us -> 1.92 us  [on_device(): part = keep + permute(send, perm=swap_pairs())]
    all_to_all x1, blocking collectives: 33.1 us -> 30 us  [on_device(): lax.all_to_all(part.reshape(16, TILE // 8, TILE), ('depth', 'col'), 0, 0,...]
  transfers between devices with their start and end apart: 23 -> 19, of which waited for: 9 -> 6; matrix products, arithmetic and copies ran while one was open for 0% -> 0% of each run, Pallas kernels for 0% -> 0%
where the time goes in v2:
time: 127 us; the launch traced here: 126 us
  starting transfers between devices  51.1 us (40%)
  blocking collectives  45.6 us (36%)
  waiting for transfers between devices  21.4 us (17%)
  other arithmetic  2.96 us (2%)
  Pallas kernels  2.63 us (2%)
  between operations  1.62 us (1%)
    all_to_all x1, blocking collectives, on_device(): lax.all_to_all(part.reshape(16, TILE // 8, TILE), ('depth', 'col'), 0, 0,...  30 us
    ppermute x3, starting transfers between devices, on_device(): left = permute(left, perm=z_pairs(step, -1))  19.1 us
    all_to_all x1, blocking collectives, on_device(): return lax.all_to_all(spread, 'depth', 0, 0).reshape(TILE, TILE)  15.5 us
    ppermute x4, starting transfers between devices, on_device(): first.append(permute(first[-1], perm=y_pairs(step, 4)))  9.98 us
    ppermute x4, starting transfers between devices, on_device(): right = permute(right, perm=z_pairs(step, 1))  9.12 us
    ppermute x3, waiting for transfers between devices, on_device(): left = permute(left, perm=z_pairs(step, -1))  6.31 us
    ppermute x4, waiting for transfers between devices, on_device(): first.append(permute(first[-1], perm=y_pairs(step, 4)))  5.95 us
    ppermute x3, starting transfers between devices, on_device(): second = permute(second, perm=y_pairs(step, 3))  5.59 us
  transfers between devices with their start and end apart: 19, of which 6 were waited for; matrix products, arithmetic and copies ran while one was open for 0% of the time, Pallas kernels for 0%

profile of v2, /device:TPU:2, one launch (start us, length us, event | category | flops | bytes accessed | tf_op | source)
XLA Modules:
  0.0 126.2 jit_solution(8144186012136691137)
XLA Ops:
  1.3 0.7 fusion.1
  2.0 0.9 subtract_reduce_fusion
  2.9 0.1 broadcast_in_dim.15
  3.0 0.1 broadcast_in_dim.29
  3.0 0.0 copy-start.1
  3.0 1.2 pad_maximum_fusion
  4.2 0.0 copy-start
  4.3 2.1 %collective-permute-start = (bf16[1568,256]{1,0:T(8,128)(2,1)S(1)}, bf16[1568,256]{1,0:T(8,128)(2,1)S(1)}, u32[]{:S(2)}, u32[]{:S(2)}) collective-permute-start(bf16[1568,256]{1,0:T(8,128)(2,1)S(1)} %pad_maximum_fusion), channel_id=1, source_target_pairs={{0,16},{1,17},{2,18},{3,19},{4,20},{5,21},{6,22},{7,23},{16,0},{17... | collective-permute-start | bytes 2408456 | tf_op jit(solution)/shard_map/pair/ppermute | solution.py:185
  6.3 2.3 %collective-permute-done = bf16[1568,256]{1,0:T(8,128)(2,1)S(1)} collective-permute-done((bf16[1568,256]{1,0:T(8,128)(2,1)S(1)}, bf16[1568,256]{1,0:T(8,128)(2,1)S(1)}, u32[]{:S(2)}, u32[]{:S(2)}) %collective-permute-start) | collective-permute-done | bytes 802848 | tf_op jit(solution)/shard_map/pair/ppermute | solution.py:185
  8.6 0.0 copy-done.1
  8.7 5.2 %collective-permute-start.1 = (bf16[1056,256]{1,0:T(8,128)(2,1)S(1)}, bf16[1056,256]{1,0:T(8,128)(2,1)S(1)}, u32[]{:S(2)}, u32[]{:S(2)}) collective-permute-start(bf16[1056,256]{1,0:T(8,128)(2,1)S(1)} %pad_maximum_fusion.1.refs_0_), channel_id=1, source_target_pairs={{0,1},{1,2},{4,5},{5,6},{18,19},{19,20},{22,23},{23,16},{32,33},{3... | collective-permute-start | bytes 1622024 | tf_op jit(solution)/shard_map/ring_matrix/ppermute | solution.py:201
  13.9 0.0 copy-done
  14.0 3.6 %collective-permute-start.8 = (bf16[1040,256]{1,0:T(8,128)(2,1)S(1)}, bf16[1040,256]{1,0:T(8,128)(2,1)S(1)}, u32[]{:S(2)}, u32[]{:S(2)}) collective-permute-start(bf16[1040,256]{1,0:T(8,128)(2,1)S(1)} %pad_maximum_fusion.2.refs_8_), channel_id=1, source_target_pairs={{0,32},{1,33},{2,34},{3,35},{4,36},{5,37},{6,38},{7,39},{32,64},{3... | collective-permute-start | bytes 1597448 | tf_op jit(solution)/shard_map/ring_square/ppermute | solution.py:196
  17.6 3.6 %collective-permute-start.12 = (bf16[1040,256]{1,0:T(8,128)(2,1)S(1)}, bf16[1040,256]{1,0:T(8,128)(2,1)S(1)}, u32[]{:S(2)}, u32[]{:S(2)}) collective-permute-start(bf16[1040,256]{1,0:T(8,128)(2,1)S(1)} %slice.17), channel_id=1, source_target_pairs={{0,32},{1,33},{2,34},{3,35},{4,36},{5,37},{6,38},{7,39},{32,64},{3... | collective-permute-start | bytes 1597448 | tf_op jit(solution)/shard_map/ring_square/ppermute | solution.py:198
  21.2 12.8 %collective-permute-start.5 = (bf16[1056,256]{1,0:T(8,128)(2,1)S(1)}, bf16[1056,256]{1,0:T(8,128)(2,1)S(1)}, u32[]{:S(2)}, u32[]{:S(2)}) collective-permute-start(bf16[1056,256]{1,0:T(8,128)(2,1)S(1)} %pad_maximum_fusion.1.refs_0_), channel_id=1, source_target_pairs={{0,7},{1,0},{4,3},{5,4},{18,17},{19,18},{22,21},{23,22},{32,39},{3... | collective-permute-start | bytes 1622024 | tf_op jit(solution)/shard_map/ring_matrix/ppermute | solution.py:204
  34.0 0.0 collective-permute-done.1.refs_1_
  34.0 0.7 collective-permute-start.2
  34.8 0.0 collective-permute-done.8.refs_9_
  34.8 0.7 collective-permute-start.9
  35.5 0.0 collective-permute-done.12
  35.5 0.7 collective-permute-start.14
  36.2 4.7 %collective-permute-done.5.refs_7_ = bf16[1056,256]{1,0:T(8,128)(2,1)S(1)} collective-permute-done((bf16[1056,256]{1,0:T(8,128)(2,1)S(1)}, bf16[1056,256]{1,0:T(8,128)(2,1)S(1)}, u32[]{:S(2)}, u32[]{:S(2)}) %collective-permute-start.5) | collective-permute-done | bytes 540704 | tf_op jit(solution)/shard_map/ring_matrix/ppermute | solution.py:204
  40.9 5.6 %collective-permute-start.6 = (bf16[1056,256]{1,0:T(8,128)(2,1)S(1)}, bf16[1056,256]{1,0:T(8,128)(2,1)S(1)}, u32[]{:S(2)}, u32[]{:S(2)}) collective-permute-start(bf16[1056,256]{1,0:T(8,128)(2,1)S(1)} %collective-permute-done.5.refs_7_), channel_id=1, source_target_pairs={{0,7},{3,2},{4,3},{7,6},{17,16},{18,17},{21,20},{22,21},{32,39},{3... | collective-permute-start | bytes 1622024 | tf_op jit(solution)/shard_map/ring_matrix/ppermute | solution.py:204
  46.5 0.0 collective-permute-done.2.refs_2_
  46.5 1.3 %collective-permute-start.3 = (bf16[1056,256]{1,0:T(8,128)(2,1)S(1)}, bf16[1056,256]{1,0:T(8,128)(2,1)S(1)}, u32[]{:S(2)}, u32[]{:S(2)}) collective-permute-start(bf16[1056,256]{1,0:T(8,128)(2,1)S(1)} %collective-permute-done.2.refs_2_), channel_id=1, source_target_pairs={{2,3},{3,4},{6,7},{7,0},{16,17},{17,18},{20,21},{21,22},{34,35},{3... | collective-permute-start | bytes 1622024 | tf_op jit(solution)/shard_map/ring_matrix/ppermute | solution.py:201
  47.8 0.0 collective-permute-done.9.refs_10_
  47.8 1.3 %collective-permute-start.10 = (bf16[1040,256]{1,0:T(8,128)(2,1)S(1)}, bf16[1040,256]{1,0:T(8,128)(2,1)S(1)}, u32[]{:S(2)}, u32[]{:S(2)}) collective-permute-start(bf16[1040,256]{1,0:T(8,128)(2,1)S(1)} %collective-permute-done.9.refs_10_), channel_id=1, source_target_pairs={{16,120},{17,121},{18,122},{19,123},{20,124},{21,125},{22,126},{23... | collective-permute-start | bytes 1597448 | tf_op jit(solution)/shard_map/ring_square/ppermute | solution.py:196
  49.1 1.3 %collective-permute-start.13 = (bf16[1040,256]{1,0:T(8,128)(2,1)S(1)}, bf16[1040,256]{1,0:T(8,128)(2,1)S(1)}, u32[]{:S(2)}, u32[]{:S(2)}) collective-permute-start(bf16[1040,256]{1,0:T(8,128)(2,1)S(1)} %collective-permute-done.12), channel_id=1, source_target_pairs={{16,0},{17,1},{18,2},{19,3},{20,4},{21,5},{22,6},{23,7},{32,48},{3... | collective-permute-start | bytes 1597448 | tf_op jit(solution)/shard_map/ring_square/ppermute | solution.py:199
  50.4 0.0 collective-permute-done.14
  50.5 1.3 %collective-permute-start.16 = (bf16[1040,256]{1,0:T(8,128)(2,1)S(1)}, bf16[1040,256]{1,0:T(8,128)(2,1)S(1)}, u32[]{:S(2)}, u32[]{:S(2)}) collective-permute-start(bf16[1040,256]{1,0:T(8,128)(2,1)S(1)} %collective-permute-done.14), channel_id=1, source_target_pairs={{16,120},{17,121},{18,122},{19,123},{20,124},{21,125},{22,126},{23... | collective-permute-start | bytes 1597448 | tf_op jit(solution)/shard_map/ring_square/ppermute | solution.py:198
  51.8 1.6 %collective-permute-done.6.refs_6_ = bf16[1056,256]{1,0:T(8,128)(2,1)S(1)} collective-permute-done((bf16[1056,256]{1,0:T(8,128)(2,1)S(1)}, bf16[1056,256]{1,0:T(8,128)(2,1)S(1)}, u32[]{:S(2)}, u32[]{:S(2)}) %collective-permute-start.6) | collective-permute-done | bytes 540704 | tf_op jit(solution)/shard_map/ring_matrix/ppermute | solution.py:204
  53.3 0.7 collective-permute-start.7
  54.0 5.0 %collective-permute-done.3.refs_3_ = bf16[1056,256]{1,0:T(8,128)(2,1)S(1)} collective-permute-done((bf16[1056,256]{1,0:T(8,128)(2,1)S(1)}, bf16[1056,256]{1,0:T(8,128)(2,1)S(1)}, u32[]{:S(2)}, u32[]{:S(2)}) %collective-permute-start.3) | collective-permute-done | bytes 540704 | tf_op jit(solution)/shard_map/ring_matrix/ppermute | solution.py:201
  59.0 1.9 %collective-permute-start.4 = (bf16[1056,256]{1,0:T(8,128)(2,1)S(1)}, bf16[1056,256]{1,0:T(8,128)(2,1)S(1)}, u32[]{:S(2)}, u32[]{:S(2)}) collective-permute-start(bf16[1056,256]{1,0:T(8,128)(2,1)S(1)} %collective-permute-done.3.refs_3_), channel_id=1, source_target_pairs={{0,1},{3,4},{4,5},{7,0},{17,18},{18,19},{21,22},{22,23},{32,33},{3... | collective-permute-start | bytes 1622024 | tf_op jit(solution)/shard_map/ring_matrix/ppermute | solution.py:201
  60.9 0.0 collective-permute-done.10.refs_11_
  60.9 4.4 %collective-permute-start.11 = (bf16[1040,256]{1,0:T(8,128)(2,1)S(1)}, bf16[1040,256]{1,0:T(8,128)(2,1)S(1)}, u32[]{:S(2)}, u32[]{:S(2)}) collective-permute-start(bf16[1040,256]{1,0:T(8,128)(2,1)S(1)} %collective-permute-done.10.refs_11_), channel_id=1, source_target_pairs={{0,32},{1,33},{2,34},{3,35},{4,36},{5,37},{6,38},{7,39},{16,120},{... | collective-permute-start | bytes 1597448 | tf_op jit(solution)/shard_map/ring_square/ppermute | solution.py:196
  65.3 0.0 collective-permute-done.13.refs_13_
  65.3 0.7 collective-permute-start.15
  66.0 0.0 collective-permute-done.16
  66.0 1.3 %collective-permute-start.17 = (bf16[1040,256]{1,0:T(8,128)(2,1)S(1)}, bf16[1040,256]{1,0:T(8,128)(2,1)S(1)}, u32[]{:S(2)}, u32[]{:S(2)}) collective-permute-start(bf16[1040,256]{1,0:T(8,128)(2,1)S(1)} %collective-permute-done.16), channel_id=1, source_target_pairs={{0,16},{1,17},{2,18},{3,19},{4,20},{5,21},{6,22},{7,23},{48,32},{4... | collective-permute-start | bytes 1597448 | tf_op jit(solution)/shard_map/ring_square/ppermute | solution.py:199
  67.3 5.9 %collective-permute-done.11.refs_12_ = bf16[1040,256]{1,0:T(8,128)(2,1)S(1)} collective-permute-done((bf16[1040,256]{1,0:T(8,128)(2,1)S(1)}, bf16[1040,256]{1,0:T(8,128)(2,1)S(1)}, u32[]{:S(2)}, u32[]{:S(2)}) %collective-permute-start.11) | collective-permute-done | bytes 532512 | tf_op jit(solution)/shard_map/ring_square/ppermute | solution.py:196
  73.3 0.0 collective-permute-done.15.refs_14_
  73.3 0.0 collective-permute-done.7.refs_5_
  73.3 0.0 collective-permute-done.17.refs_15_
  73.3 0.0 collective-permute-done.4.refs_4_
  73.3 2.6 %shard_map.64 = (f32[2,256,256]{2,1,0:T(8,128)S(1)}, f32[2,256,256]{2,1,0:T(8,128)S(1)}) custom-call(bf16[1056,256]{1,0:T(8,128)(2,1)S(1)} %pad_maximum_fusion.1.refs_0_, bf16[1056,256]{1,0:T(8,128)(2,1)S(1)} %collective-permute-done.1.refs_1_, bf16[1056,256]{1,0:T(8,128)(2,1)S(1)} %collective-permute-done.2.refs_2_, ...), custom_call_target="tpu_custom_call" | custom-call | flops 268435456 | bytes 5242880 | tf_op jit(solution)/shard_map/pallas_call | solution.py:151
  76.0 1.9 %collective-permute-start.18 = (f32[2,256,256]{2,1,0:T(8,128)S(1)}, f32[2,256,256]{2,1,0:T(8,128)S(1)}, u32[]{:S(2)}, u32[]{:S(2)}) collective-permute-start(f32[2,256,256]{2,1,0:T(8,128)S(1)} %get-tuple-element.8), channel_id=1, source_target_pairs={{0,16},{1,17},{2,18},{3,19},{4,20},{5,21},{6,22},{7,23},{16,0},{17... | collective-permute-start | bytes 1572872 | tf_op jit(solution)/shard_map/pair_sum/ppermute | solution.py:209
  77.9 1.9 %collective-permute-done.18 = f32[2,256,256]{2,1,0:T(8,128)S(1)} collective-permute-done((f32[2,256,256]{2,1,0:T(8,128)S(1)}, f32[2,256,256]{2,1,0:T(8,128)S(1)}, u32[]{:S(2)}, u32[]{:S(2)}) %collective-permute-start.18) | collective-permute-done | bytes 524320 | tf_op jit(solution)/shard_map/pair_sum/ppermute | solution.py:209
  79.8 0.1 add.7
  79.8 30.0 %all_to_all.10 = f32[16,32,256]{2,1,0:T(8,128)S(1)} all-to-all(f32[16,32,256]{2,1,0:T(8,128)S(1)} %bitcast.12), channel_id=1, replica_groups={{0,128,256,384,512,640,768,896,8,136,264,392,520,648,776,904},{1,129,25..., dimensions={0} | all-to-all | bytes 1048576 | tf_op jit(solution)/shard_map/scatter_sum/all_to_all | solution.py:214
  109.9 15.5 %all_to_all.11 = f32[8,32,256]{2,1,0:T(8,128)S(1)} all-to-all(f32[8,32,256]{2,1,0:T(8,128)S(1)} %broadcast_in_dim.30), channel_id=1, replica_groups=mesh['depth'=8,'row'=8,'col'=16] {'depth'}, dimensions={0} | all-to-all | bytes 524288 | tf_op jit(solution)/shard_map/gather_rows/all_to_all | solution.py:220
  125.5 0.7 copy.10
  (10 shorter events, 0.2 us)
Async XLA Ops:
  3.0 5.6 %copy-start.1 = (bf16[2,256,256]{2,1,0:T(8,128)(2,1)S(1)}, bf16[2,256,256]{2,1,0:T(8,128)(2,1)}, u32[]{:S(2)}) copy-start(bf16[2,256,256]{2,1,0:T(8,128)(2,1)} %param.6) | copy-start | bytes 786436
  4.2 9.7 %copy-start = (bf16[4,256,256]{2,1,0:T(8,128)(2,1)S(1)}, bf16[4,256,256]{2,1,0:T(8,128)(2,1)}, u32[]{:S(2)}) copy-start(bf16[4,256,256]{2,1,0:T(8,128)(2,1)} %param.9) | copy-start | bytes 1572868
  4.3 4.3 %collective-permute-start = (bf16[1568,256]{1,0:T(8,128)(2,1)S(1)}, bf16[1568,256]{1,0:T(8,128)(2,1)S(1)}, u32[]{:S(2)}, u32[]{:S(2)}) collective-permute-start(bf16[1568,256]{1,0:T(8,128)(2,1)S(1)} %pad_maximum_fusion), channel_id=1, source_target_pairs={{0,16},{1,17},{2,18},{3,19},{4,20},{5,21},{6,22},{7,23},{16,0},{17... | collective-permute-start | bytes 2408456 | tf_op jit(solution)/shard_map/pair/ppermute | solution.py:185
  8.7 25.4 %collective-permute-start.1 = (bf16[1056,256]{1,0:T(8,128)(2,1)S(1)}, bf16[1056,256]{1,0:T(8,128)(2,1)S(1)}, u32[]{:S(2)}, u32[]{:S(2)}) collective-permute-start(bf16[1056,256]{1,0:T(8,128)(2,1)S(1)} %pad_maximum_fusion.1.refs_0_), channel_id=1, source_target_pairs={{0,1},{1,2},{4,5},{5,6},{18,19},{19,20},{22,23},{23,16},{32,33},{3... | collective-permute-start | bytes 1622024 | tf_op jit(solution)/shard_map/ring_matrix/ppermute | solution.py:201
  14.0 20.8 %collective-permute-start.8 = (bf16[1040,256]{1,0:T(8,128)(2,1)S(1)}, bf16[1040,256]{1,0:T(8,128)(2,1)S(1)}, u32[]{:S(2)}, u32[]{:S(2)}) collective-permute-start(bf16[1040,256]{1,0:T(8,128)(2,1)S(1)} %pad_maximum_fusion.2.refs_8_), channel_id=1, source_target_pairs={{0,32},{1,33},{2,34},{3,35},{4,36},{5,37},{6,38},{7,39},{32,64},{3... | collective-permute-start | bytes 1597448 | tf_op jit(solution)/shard_map/ring_square/ppermute | solution.py:196
  17.6 17.8 %collective-permute-start.12 = (bf16[1040,256]{1,0:T(8,128)(2,1)S(1)}, bf16[1040,256]{1,0:T(8,128)(2,1)S(1)}, u32[]{:S(2)}, u32[]{:S(2)}) collective-permute-start(bf16[1040,256]{1,0:T(8,128)(2,1)S(1)} %slice.17), channel_id=1, source_target_pairs={{0,32},{1,33},{2,34},{3,35},{4,36},{5,37},{6,38},{7,39},{32,64},{3... | collective-permute-start | bytes 1597448 | tf_op jit(solution)/shard_map/ring_square/ppermute | solution.py:198
  21.2 19.7 %collective-permute-start.5 = (bf16[1056,256]{1,0:T(8,128)(2,1)S(1)}, bf16[1056,256]{1,0:T(8,128)(2,1)S(1)}, u32[]{:S(2)}, u32[]{:S(2)}) collective-permute-start(bf16[1056,256]{1,0:T(8,128)(2,1)S(1)} %pad_maximum_fusion.1.refs_0_), channel_id=1, source_target_pairs={{0,7},{1,0},{4,3},{5,4},{18,17},{19,18},{22,21},{23,22},{32,39},{3... | collective-permute-start | bytes 1622024 | tf_op jit(solution)/shard_map/ring_matrix/ppermute | solution.py:204
  34.0 12.5 %collective-permute-start.2 = (bf16[1056,256]{1,0:T(8,128)(2,1)S(1)}, bf16[1056,256]{1,0:T(8,128)(2,1)S(1)}, u32[]{:S(2)}, u32[]{:S(2)}) collective-permute-start(bf16[1056,256]{1,0:T(8,128)(2,1)S(1)} %collective-permute-done.1.refs_1_), channel_id=1, source_target_pairs={{1,2},{2,3},{5,6},{6,7},{16,17},{19,20},{20,21},{23,16},{33,34},{3... | collective-permute-start | bytes 1622024 | tf_op jit(solution)/shard_map/ring_matrix/ppermute | solution.py:201
  34.8 13.1 %collective-permute-start.9 = (bf16[1040,256]{1,0:T(8,128)(2,1)S(1)}, bf16[1040,256]{1,0:T(8,128)(2,1)S(1)}, u32[]{:S(2)}, u32[]{:S(2)}) collective-permute-start(bf16[1040,256]{1,0:T(8,128)(2,1)S(1)} %collective-permute-done.8.refs_9_), channel_id=1, source_target_pairs={{32,64},{33,65},{34,66},{35,67},{36,68},{37,69},{38,70},{39,71},{4... | collective-permute-start | bytes 1597448 | tf_op jit(solution)/shard_map/ring_square/ppermute | solution.py:196
  35.5 15.0 %collective-permute-start.14 = (bf16[1040,256]{1,0:T(8,128)(2,1)S(1)}, bf16[1040,256]{1,0:T(8,128)(2,1)S(1)}, u32[]{:S(2)}, u32[]{:S(2)}) collective-permute-start(bf16[1040,256]{1,0:T(8,128)(2,1)S(1)} %collective-permute-done.12), channel_id=1, source_target_pairs={{32,64},{33,65},{34,66},{35,67},{36,68},{37,69},{38,70},{39,71},{4... | collective-permute-start | bytes 1597448 | tf_op jit(solution)/shard_map/ring_square/ppermute | solution.py:198
  40.9 12.4 %collective-permute-start.6 = (bf16[1056,256]{1,0:T(8,128)(2,1)S(1)}, bf16[1056,256]{1,0:T(8,128)(2,1)S(1)}, u32[]{:S(2)}, u32[]{:S(2)}) collective-permute-start(bf16[1056,256]{1,0:T(8,128)(2,1)S(1)} %collective-permute-done.5.refs_7_), channel_id=1, source_target_pairs={{0,7},{3,2},{4,3},{7,6},{17,16},{18,17},{21,20},{22,21},{32,39},{3... | collective-permute-start | bytes 1622024 | tf_op jit(solution)/shard_map/ring_matrix/ppermute | solution.py:204
  46.5 12.5 %collective-permute-start.3 = (bf16[1056,256]{1,0:T(8,128)(2,1)S(1)}, bf16[1056,256]{1,0:T(8,128)(2,1)S(1)}, u32[]{:S(2)}, u32[]{:S(2)}) collective-permute-start(bf16[1056,256]{1,0:T(8,128)(2,1)S(1)} %collective-permute-done.2.refs_2_), channel_id=1, source_target_pairs={{2,3},{3,4},{6,7},{7,0},{16,17},{17,18},{20,21},{21,22},{34,35},{3... | collective-permute-start | bytes 1622024 | tf_op jit(solution)/shard_map/ring_matrix/ppermute | solution.py:201
  47.8 13.1 %collective-permute-start.10 = (bf16[1040,256]{1,0:T(8,128)(2,1)S(1)}, bf16[1040,256]{1,0:T(8,128)(2,1)S(1)}, u32[]{:S(2)}, u32[]{:S(2)}) collective-permute-start(bf16[1040,256]{1,0:T(8,128)(2,1)S(1)} %collective-permute-done.9.refs_10_), channel_id=1, source_target_pairs={{16,120},{17,121},{18,122},{19,123},{20,124},{21,125},{22,126},{23... | collective-permute-start | bytes 1597448 | tf_op jit(solution)/shard_map/ring_square/ppermute | solution.py:196
  49.1 16.2 %collective-permute-start.13 = (bf16[1040,256]{1,0:T(8,128)(2,1)S(1)}, bf16[1040,256]{1,0:T(8,128)(2,1)S(1)}, u32[]{:S(2)}, u32[]{:S(2)}) collective-permute-start(bf16[1040,256]{1,0:T(8,128)(2,1)S(1)} %collective-permute-done.12), channel_id=1, source_target_pairs={{16,0},{17,1},{18,2},{19,3},{20,4},{21,5},{22,6},{23,7},{32,48},{3... | collective-permute-start | bytes 1597448 | tf_op jit(solution)/shard_map/ring_square/ppermute | solution.py:199
  50.5 15.6 %collective-permute-start.16 = (bf16[1040,256]{1,0:T(8,128)(2,1)S(1)}, bf16[1040,256]{1,0:T(8,128)(2,1)S(1)}, u32[]{:S(2)}, u32[]{:S(2)}) collective-permute-start(bf16[1040,256]{1,0:T(8,128)(2,1)S(1)} %collective-permute-done.14), channel_id=1, source_target_pairs={{16,120},{17,121},{18,122},{19,123},{20,124},{21,125},{22,126},{23... | collective-permute-start | bytes 1597448 | tf_op jit(solution)/shard_map/ring_square/ppermute | solution.py:198
  53.3 20.0 %collective-permute-start.7 = (bf16[1056,256]{1,0:T(8,128)(2,1)S(1)}, bf16[1056,256]{1,0:T(8,128)(2,1)S(1)}, u32[]{:S(2)}, u32[]{:S(2)}) collective-permute-start(bf16[1056,256]{1,0:T(8,128)(2,1)S(1)} %collective-permute-done.6.refs_6_), channel_id=1, source_target_pairs={{2,1},{3,2},{6,5},{7,6},{16,23},{17,16},{20,19},{21,20},{34,33},{3... | collective-permute-start | bytes 1622024 | tf_op jit(solution)/shard_map/ring_matrix/ppermute | solution.py:204
  59.0 14.3 %collective-permute-start.4 = (bf16[1056,256]{1,0:T(8,128)(2,1)S(1)}, bf16[1056,256]{1,0:T(8,128)(2,1)S(1)}, u32[]{:S(2)}, u32[]{:S(2)}) collective-permute-start(bf16[1056,256]{1,0:T(8,128)(2,1)S(1)} %collective-permute-done.3.refs_3_), channel_id=1, source_target_pairs={{0,1},{3,4},{4,5},{7,0},{17,18},{18,19},{21,22},{22,23},{32,33},{3... | collective-permute-start | bytes 1622024 | tf_op jit(solution)/shard_map/ring_matrix/ppermute | solution.py:201
  60.9 12.4 %collective-permute-start.11 = (bf16[1040,256]{1,0:T(8,128)(2,1)S(1)}, bf16[1040,256]{1,0:T(8,128)(2,1)S(1)}, u32[]{:S(2)}, u32[]{:S(2)}) collective-permute-start(bf16[1040,256]{1,0:T(8,128)(2,1)S(1)} %collective-permute-done.10.refs_11_), channel_id=1, source_target_pairs={{0,32},{1,33},{2,34},{3,35},{4,36},{5,37},{6,38},{7,39},{16,120},{... | collective-permute-start | bytes 1597448 | tf_op jit(solution)/shard_map/ring_square/ppermute | solution.py:196
  65.3 8.0 %collective-permute-start.15 = (bf16[1040,256]{1,0:T(8,128)(2,1)S(1)}, bf16[1040,256]{1,0:T(8,128)(2,1)S(1)}, u32[]{:S(2)}, u32[]{:S(2)}) collective-permute-start(bf16[1040,256]{1,0:T(8,128)(2,1)S(1)} %collective-permute-done.14), channel_id=1, source_target_pairs={{64,80},{65,81},{66,82},{67,83},{68,84},{69,85},{70,86},{71,87},{8... | collective-permute-start | bytes 1597448 | tf_op jit(solution)/shard_map/ring_square/ppermute | solution.py:199
  66.0 7.3 %collective-permute-start.17 = (bf16[1040,256]{1,0:T(8,128)(2,1)S(1)}, bf16[1040,256]{1,0:T(8,128)(2,1)S(1)}, u32[]{:S(2)}, u32[]{:S(2)}) collective-permute-start(bf16[1040,256]{1,0:T(8,128)(2,1)S(1)} %collective-permute-done.16), channel_id=1, source_target_pairs={{0,16},{1,17},{2,18},{3,19},{4,20},{5,21},{6,22},{7,23},{48,32},{4... | collective-permute-start | bytes 1597448 | tf_op jit(solution)/shard_map/ring_square/ppermute | solution.py:199
  76.0 3.8 %collective-permute-start.18 = (f32[2,256,256]{2,1,0:T(8,128)S(1)}, f32[2,256,256]{2,1,0:T(8,128)S(1)}, u32[]{:S(2)}, u32[]{:S(2)}) collective-permute-start(f32[2,256,256]{2,1,0:T(8,128)S(1)} %get-tuple-element.8), channel_id=1, source_target_pairs={{0,16},{1,17},{2,18},{3,19},{4,20},{5,21},{6,22},{7,23},{16,0},{17... | collective-permute-start | bytes 1572872 | tf_op jit(solution)/shard_map/pair_sum/ppermute | solution.py:209

commit v3 on v2

--- a/solution.py
+++ b/solution.py
@@ -131,15 +131,16 @@
                 @pl.when((key >= 0) & (match >= 0))
                 def _():
                     q_start = pl.multiple_of(match * TILE, 16)
-                    out_ref[b] += jnp.dot(
+                    out_ref[:, b] += jnp.dot(
                         x_buf[slot, pl.ds(start, TILE), :],
                         q_buf[place, pl.ds(q_start, TILE), :],
                         preferred_element_type=jnp.float32,
-                    )
+                    ).reshape(8, TILE // 8, TILE)
 
             @pl.when((key >= 0) & (layer == 0) & (y_hi == 0) & (k4 == 0) & (inner == z))
             def _():
-                out_ref[core] -= 3.0 * x_buf[slot, pl.ds(start, TILE), :].astype(jnp.float32)
+                diagonal = x_buf[slot, pl.ds(start, TILE), :].astype(jnp.float32)
+                out_ref[:, core] -= 3.0 * diagonal.reshape(8, TILE // 8, TILE)
 
             return carry
 
@@ -147,7 +148,7 @@
 
 
 def products(x_pieces, q_pieces):
-    block = jax.ShapeDtypeStruct((2, TILE, TILE), jnp.float32)
+    block = jax.ShapeDtypeStruct((8, 2, TILE // 8, TILE), jnp.float32)
     return pl.pallas_call(
         product_kernel,
         out_shape=(block, block),
@@ -209,7 +210,7 @@
         part = keep + permute(send, perm=swap_pairs())
     with jax.named_scope("scatter_sum"):
         groups = [
-            [layer * 16 + y_hi * 8 + z for y_hi in range(2) for layer in range(8)] for z in range(8)
+            [layer * 16 + y_hi * 8 + z for layer in range(8) for y_hi in range(2)] for z in range(8)
         ]
         shares = lax.all_to_all(
             part.reshape(16, TILE // 8, TILE), ("depth", "col"), 0, 0, axis_index_groups=groups

time: 127 us -> 131 us (1.031)
  blocking collectives: 45.6 us -> 49 us
    all_to_all x1, blocking collectives: 30 us -> 31.8 us  [on_device(): lax.all_to_all(part.reshape(16, TILE // 8, TILE), ('depth', 'col'), 0, 0,...]
    all_to_all x1, blocking collectives: 15.5 us -> 17.2 us  [on_device(): return lax.all_to_all(spread, 'depth', 0, 0).reshape(TILE, TILE)]
where the time goes in v3:
time: 131 us; the launch traced here: 130 us
  starting transfers between devices  51.1 us (39%)
  blocking collectives  49 us (37%)
  waiting for transfers between devices  21.4 us (16%)
  other arithmetic  2.97 us (2%)
  Pallas kernels  2.81 us (2%)
  between operations  1.62 us (1%)
    all_to_all x1, blocking collectives, on_device(): lax.all_to_all(part.reshape(16, TILE // 8, TILE), ('depth', 'col'), 0, 0,...  31.8 us
    ppermute x3, starting transfers between devices, on_device(): left = permute(left, perm=z_pairs(step, -1))  19.1 us
    all_to_all x1, blocking collectives, on_device(): return lax.all_to_all(spread, 'depth', 0, 0).reshape(TILE, TILE)  17.2 us
    ppermute x4, starting transfers between devices, on_device(): first.append(permute(first[-1], perm=y_pairs(step, 4)))  9.98 us
    ppermute x4, starting transfers between devices, on_device(): right = permute(right, perm=z_pairs(step, 1))  9.12 us
    ppermute x3, waiting for transfers between devices, on_device(): left = permute(left, perm=z_pairs(step, -1))  6.31 us
    ppermute x4, waiting for transfers between devices, on_device(): first.append(permute(first[-1], perm=y_pairs(step, 4)))  5.95 us
    ppermute x3, starting transfers between devices, on_device(): second = permute(second, perm=y_pairs(step, 3))  5.59 us
  transfers between devices with their start and end apart: 19, of which 6 were waited for; matrix products, arithmetic and copies ran while one was open for 0% of the time, Pallas kernels for 0%

profile of v3, /device:TPU:2, one launch (start us, length us, event | category | flops | bytes accessed | tf_op | source)
XLA Modules:
  0.0 129.8 jit_solution(17696436187528689598)
XLA Ops:
  1.3 0.7 fusion.1
  2.0 0.9 subtract_reduce_fusion
  2.9 0.1 broadcast_in_dim.15
  3.0 0.1 broadcast_in_dim.29
  3.0 0.0 copy-start.1
  3.0 1.2 pad_maximum_fusion
  4.2 0.0 copy-start
  4.3 2.1 %collective-permute-start = (bf16[1568,256]{1,0:T(8,128)(2,1)S(1)}, bf16[1568,256]{1,0:T(8,128)(2,1)S(1)}, u32[]{:S(2)}, u32[]{:S(2)}) collective-permute-start(bf16[1568,256]{1,0:T(8,128)(2,1)S(1)} %pad_maximum_fusion), channel_id=1, source_target_pairs={{0,16},{1,17},{2,18},{3,19},{4,20},{5,21},{6,22},{7,23},{16,0},{17... | collective-permute-start | bytes 2408456 | tf_op jit(solution)/shard_map/pair/ppermute | solution.py:186
  6.3 2.3 %collective-permute-done = bf16[1568,256]{1,0:T(8,128)(2,1)S(1)} collective-permute-done((bf16[1568,256]{1,0:T(8,128)(2,1)S(1)}, bf16[1568,256]{1,0:T(8,128)(2,1)S(1)}, u32[]{:S(2)}, u32[]{:S(2)}) %collective-permute-start) | collective-permute-done | bytes 802848 | tf_op jit(solution)/shard_map/pair/ppermute | solution.py:186
  8.6 0.0 copy-done.1
  8.7 5.2 %collective-permute-start.1 = (bf16[1056,256]{1,0:T(8,128)(2,1)S(1)}, bf16[1056,256]{1,0:T(8,128)(2,1)S(1)}, u32[]{:S(2)}, u32[]{:S(2)}) collective-permute-start(bf16[1056,256]{1,0:T(8,128)(2,1)S(1)} %pad_maximum_fusion.1.refs_0_), channel_id=1, source_target_pairs={{0,1},{1,2},{4,5},{5,6},{18,19},{19,20},{22,23},{23,16},{32,33},{3... | collective-permute-start | bytes 1622024 | tf_op jit(solution)/shard_map/ring_matrix/ppermute | solution.py:202
  13.9 0.0 copy-done
  14.0 3.6 %collective-permute-start.8 = (bf16[1040,256]{1,0:T(8,128)(2,1)S(1)}, bf16[1040,256]{1,0:T(8,128)(2,1)S(1)}, u32[]{:S(2)}, u32[]{:S(2)}) collective-permute-start(bf16[1040,256]{1,0:T(8,128)(2,1)S(1)} %pad_maximum_fusion.2.refs_8_), channel_id=1, source_target_pairs={{0,32},{1,33},{2,34},{3,35},{4,36},{5,37},{6,38},{7,39},{32,64},{3... | collective-permute-start | bytes 1597448 | tf_op jit(solution)/shard_map/ring_square/ppermute | solution.py:197
  17.6 3.6 %collective-permute-start.12 = (bf16[1040,256]{1,0:T(8,128)(2,1)S(1)}, bf16[1040,256]{1,0:T(8,128)(2,1)S(1)}, u32[]{:S(2)}, u32[]{:S(2)}) collective-permute-start(bf16[1040,256]{1,0:T(8,128)(2,1)S(1)} %slice.17), channel_id=1, source_target_pairs={{0,32},{1,33},{2,34},{3,35},{4,36},{5,37},{6,38},{7,39},{32,64},{3... | collective-permute-start | bytes 1597448 | tf_op jit(solution)/shard_map/ring_square/ppermute | solution.py:199
  21.2 12.8 %collective-permute-start.5 = (bf16[1056,256]{1,0:T(8,128)(2,1)S(1)}, bf16[1056,256]{1,0:T(8,128)(2,1)S(1)}, u32[]{:S(2)}, u32[]{:S(2)}) collective-permute-start(bf16[1056,256]{1,0:T(8,128)(2,1)S(1)} %pad_maximum_fusion.1.refs_0_), channel_id=1, source_target_pairs={{0,7},{1,0},{4,3},{5,4},{18,17},{19,18},{22,21},{23,22},{32,39},{3... | collective-permute-start | bytes 1622024 | tf_op jit(solution)/shard_map/ring_matrix/ppermute | solution.py:205
  34.0 0.0 collective-permute-done.1.refs_1_
  34.0 0.7 collective-permute-start.2
  34.8 0.0 collective-permute-done.8.refs_9_
  34.8 0.7 collective-permute-start.9
  35.5 0.0 collective-permute-done.12
  35.5 0.7 collective-permute-start.14
  36.2 4.7 %collective-permute-done.5.refs_7_ = bf16[1056,256]{1,0:T(8,128)(2,1)S(1)} collective-permute-done((bf16[1056,256]{1,0:T(8,128)(2,1)S(1)}, bf16[1056,256]{1,0:T(8,128)(2,1)S(1)}, u32[]{:S(2)}, u32[]{:S(2)}) %collective-permute-start.5) | collective-permute-done | bytes 540704 | tf_op jit(solution)/shard_map/ring_matrix/ppermute | solution.py:205
  40.9 5.6 %collective-permute-start.6 = (bf16[1056,256]{1,0:T(8,128)(2,1)S(1)}, bf16[1056,256]{1,0:T(8,128)(2,1)S(1)}, u32[]{:S(2)}, u32[]{:S(2)}) collective-permute-start(bf16[1056,256]{1,0:T(8,128)(2,1)S(1)} %collective-permute-done.5.refs_7_), channel_id=1, source_target_pairs={{0,7},{3,2},{4,3},{7,6},{17,16},{18,17},{21,20},{22,21},{32,39},{3... | collective-permute-start | bytes 1622024 | tf_op jit(solution)/shard_map/ring_matrix/ppermute | solution.py:205
  46.5 0.0 collective-permute-done.2.refs_2_
  46.5 1.3 collective-permute-start.3
  47.8 0.0 collective-permute-done.9.refs_10_
  47.8 1.3 collective-permute-start.10
  49.1 1.3 collective-permute-start.13
  50.4 0.0 collective-permute-done.14
  50.5 1.3 collective-permute-start.16
  51.8 1.6 %collective-permute-done.6.refs_6_ = bf16[1056,256]{1,0:T(8,128)(2,1)S(1)} collective-permute-done((bf16[1056,256]{1,0:T(8,128)(2,1)S(1)}, bf16[1056,256]{1,0:T(8,128)(2,1)S(1)}, u32[]{:S(2)}, u32[]{:S(2)}) %collective-permute-start.6) | collective-permute-done | bytes 540704 | tf_op jit(solution)/shard_map/ring_matrix/ppermute | solution.py:205
  53.3 0.7 collective-permute-start.7
  54.0 5.0 %collective-permute-done.3.refs_3_ = bf16[1056,256]{1,0:T(8,128)(2,1)S(1)} collective-permute-done((bf16[1056,256]{1,0:T(8,128)(2,1)S(1)}, bf16[1056,256]{1,0:T(8,128)(2,1)S(1)}, u32[]{:S(2)}, u32[]{:S(2)}) %collective-permute-start.3) | collective-permute-done | bytes 540704 | tf_op jit(solution)/shard_map/ring_matrix/ppermute | solution.py:202
  59.0 1.9 %collective-permute-start.4 = (bf16[1056,256]{1,0:T(8,128)(2,1)S(1)}, bf16[1056,256]{1,0:T(8,128)(2,1)S(1)}, u32[]{:S(2)}, u32[]{:S(2)}) collective-permute-start(bf16[1056,256]{1,0:T(8,128)(2,1)S(1)} %collective-permute-done.3.refs_3_), channel_id=1, source_target_pairs={{0,1},{3,4},{4,5},{7,0},{17,18},{18,19},{21,22},{22,23},{32,33},{3... | collective-permute-start | bytes 1622024 | tf_op jit(solution)/shard_map/ring_matrix/ppermute | solution.py:202
  60.9 0.0 collective-permute-done.10.refs_11_
  60.9 4.4 %collective-permute-start.11 = (bf16[1040,256]{1,0:T(8,128)(2,1)S(1)}, bf16[1040,256]{1,0:T(8,128)(2,1)S(1)}, u32[]{:S(2)}, u32[]{:S(2)}) collective-permute-start(bf16[1040,256]{1,0:T(8,128)(2,1)S(1)} %collective-permute-done.10.refs_11_), channel_id=1, source_target_pairs={{0,32},{1,33},{2,34},{3,35},{4,36},{5,37},{6,38},{7,39},{16,120},{... | collective-permute-start | bytes 1597448 | tf_op jit(solution)/shard_map/ring_square/ppermute | solution.py:197
  65.3 0.0 collective-permute-done.13.refs_13_
  65.3 0.7 collective-permute-start.15
  66.0 0.0 collective-permute-done.16
  66.0 1.3 %collective-permute-start.17 = (bf16[1040,256]{1,0:T(8,128)(2,1)S(1)}, bf16[1040,256]{1,0:T(8,128)(2,1)S(1)}, u32[]{:S(2)}, u32[]{:S(2)}) collective-permute-start(bf16[1040,256]{1,0:T(8,128)(2,1)S(1)} %collective-permute-done.16), channel_id=1, source_target_pairs={{0,16},{1,17},{2,18},{3,19},{4,20},{5,21},{6,22},{7,23},{48,32},{4... | collective-permute-start | bytes 1597448 | tf_op jit(solution)/shard_map/ring_square/ppermute | solution.py:200
  67.3 5.9 %collective-permute-done.11.refs_12_ = bf16[1040,256]{1,0:T(8,128)(2,1)S(1)} collective-permute-done((bf16[1040,256]{1,0:T(8,128)(2,1)S(1)}, bf16[1040,256]{1,0:T(8,128)(2,1)S(1)}, u32[]{:S(2)}, u32[]{:S(2)}) %collective-permute-start.11) | collective-permute-done | bytes 532512 | tf_op jit(solution)/shard_map/ring_square/ppermute | solution.py:197
  73.3 0.0 collective-permute-done.15.refs_14_
  73.3 0.0 collective-permute-done.7.refs_5_
  73.3 0.0 collective-permute-done.17.refs_15_
  73.3 0.0 collective-permute-done.4.refs_4_
  73.3 2.8 %shard_map.64 = (f32[8,2,32,256]{3,2,1,0:T(8,128)S(1)}, f32[8,2,32,256]{3,2,1,0:T(8,128)S(1)}) custom-call(bf16[1056,256]{1,0:T(8,128)(2,1)S(1)} %pad_maximum_fusion.1.refs_0_, bf16[1056,256]{1,0:T(8,128)(2,1)S(1)} %collective-permute-done.1.refs_1_, bf16[1056,256]{1,0:T(8,128)(2,1)S(1)} %collective-permute-done.2.refs_2_, ...), custom_call_target="tpu_custom_call" | custom-call | flops 268435456 | bytes 5242880 | tf_op jit(solution)/shard_map/pallas_call | solution.py:152
  76.1 1.9 %collective-permute-start.18 = (f32[8,2,32,256]{3,2,1,0:T(8,128)S(1)}, f32[8,2,32,256]{3,2,1,0:T(8,128)S(1)}, u32[]{:S(2)}, u32[]{:S(2)}) collective-permute-start(f32[8,2,32,256]{3,2,1,0:T(8,128)S(1)} %get-tuple-element.8), channel_id=1, source_target_pairs={{0,16},{1,17},{2,18},{3,19},{4,20},{5,21},{6,22},{7,23},{16,0},{17... | collective-permute-start | bytes 1572872 | tf_op jit(solution)/shard_map/pair_sum/ppermute | solution.py:210
  78.1 1.9 %collective-permute-done.18 = f32[8,2,32,256]{3,2,1,0:T(8,128)S(1)} collective-permute-done((f32[8,2,32,256]{3,2,1,0:T(8,128)S(1)}, f32[8,2,32,256]{3,2,1,0:T(8,128)S(1)}, u32[]{:S(2)}, u32[]{:S(2)}) %collective-permute-start.18) | collective-permute-done | bytes 524320 | tf_op jit(solution)/shard_map/pair_sum/ppermute | solution.py:210
  79.9 0.1 add.7
  80.0 31.8 %all_to_all.10 = f32[16,32,256]{2,1,0:T(8,128)S(1)} all-to-all(f32[16,32,256]{2,1,0:T(8,128)S(1)} %bitcast.12), channel_id=1, replica_groups={{0,8,128,136,256,264,384,392,512,520,640,648,768,776,896,904},{1,9,129,..., dimensions={0} | all-to-all | bytes 1048576 | tf_op jit(solution)/shard_map/scatter_sum/all_to_all | solution.py:215
  111.9 17.2 %all_to_all.11 = f32[8,32,256]{2,1,0:T(8,128)S(1)} all-to-all(f32[8,32,256]{2,1,0:T(8,128)S(1)} %broadcast_in_dim.30), channel_id=1, replica_groups=mesh['depth'=8,'row'=8,'col'=16] {'depth'}, dimensions={0} | all-to-all | bytes 524288 | tf_op jit(solution)/shard_map/gather_rows/all_to_all | solution.py:221
  129.1 0.7 copy.10
  (10 shorter events, 0.2 us)
Async XLA Ops:
  3.0 5.6 %copy-start.1 = (bf16[2,256,256]{2,1,0:T(8,128)(2,1)S(1)}, bf16[2,256,256]{2,1,0:T(8,128)(2,1)}, u32[]{:S(2)}) copy-start(bf16[2,256,256]{2,1,0:T(8,128)(2,1)} %param.6) | copy-start | bytes 786436
  4.2 9.7 %copy-start = (bf16[4,256,256]{2,1,0:T(8,128)(2,1)S(1)}, bf16[4,256,256]{2,1,0:T(8,128)(2,1)}, u32[]{:S(2)}) copy-start(bf16[4,256,256]{2,1,0:T(8,128)(2,1)} %param.9) | copy-start | bytes 1572868
  4.3 4.3 %collective-permute-start = (bf16[1568,256]{1,0:T(8,128)(2,1)S(1)}, bf16[1568,256]{1,0:T(8,128)(2,1)S(1)}, u32[]{:S(2)}, u32[]{:S(2)}) collective-permute-start(bf16[1568,256]{1,0:T(8,128)(2,1)S(1)} %pad_maximum_fusion), channel_id=1, source_target_pairs={{0,16},{1,17},{2,18},{3,19},{4,20},{5,21},{6,22},{7,23},{16,0},{17... | collective-permute-start | bytes 2408456 | tf_op jit(solution)/shard_map/pair/ppermute | solution.py:186
  8.7 25.4 %collective-permute-start.1 = (bf16[1056,256]{1,0:T(8,128)(2,1)S(1)}, bf16[1056,256]{1,0:T(8,128)(2,1)S(1)}, u32[]{:S(2)}, u32[]{:S(2)}) collective-permute-start(bf16[1056,256]{1,0:T(8,128)(2,1)S(1)} %pad_maximum_fusion.1.refs_0_), channel_id=1, source_target_pairs={{0,1},{1,2},{4,5},{5,6},{18,19},{19,20},{22,23},{23,16},{32,33},{3... | collective-permute-start | bytes 1622024 | tf_op jit(solution)/shard_map/ring_matrix/ppermute | solution.py:202
  14.0 20.8 %collective-permute-start.8 = (bf16[1040,256]{1,0:T(8,128)(2,1)S(1)}, bf16[1040,256]{1,0:T(8,128)(2,1)S(1)}, u32[]{:S(2)}, u32[]{:S(2)}) collective-permute-start(bf16[1040,256]{1,0:T(8,128)(2,1)S(1)} %pad_maximum_fusion.2.refs_8_), channel_id=1, source_target_pairs={{0,32},{1,33},{2,34},{3,35},{4,36},{5,37},{6,38},{7,39},{32,64},{3... | collective-permute-start | bytes 1597448 | tf_op jit(solution)/shard_map/ring_square/ppermute | solution.py:197
  17.6 17.8 %collective-permute-start.12 = (bf16[1040,256]{1,0:T(8,128)(2,1)S(1)}, bf16[1040,256]{1,0:T(8,128)(2,1)S(1)}, u32[]{:S(2)}, u32[]{:S(2)}) collective-permute-start(bf16[1040,256]{1,0:T(8,128)(2,1)S(1)} %slice.17), channel_id=1, source_target_pairs={{0,32},{1,33},{2,34},{3,35},{4,36},{5,37},{6,38},{7,39},{32,64},{3... | collective-permute-start | bytes 1597448 | tf_op jit(solution)/shard_map/ring_square/ppermute | solution.py:199
  21.2 19.7 %collective-permute-start.5 = (bf16[1056,256]{1,0:T(8,128)(2,1)S(1)}, bf16[1056,256]{1,0:T(8,128)(2,1)S(1)}, u32[]{:S(2)}, u32[]{:S(2)}) collective-permute-start(bf16[1056,256]{1,0:T(8,128)(2,1)S(1)} %pad_maximum_fusion.1.refs_0_), channel_id=1, source_target_pairs={{0,7},{1,0},{4,3},{5,4},{18,17},{19,18},{22,21},{23,22},{32,39},{3... | collective-permute-start | bytes 1622024 | tf_op jit(solution)/shard_map/ring_matrix/ppermute | solution.py:205
  34.0 12.5 %collective-permute-start.2 = (bf16[1056,256]{1,0:T(8,128)(2,1)S(1)}, bf16[1056,256]{1,0:T(8,128)(2,1)S(1)}, u32[]{:S(2)}, u32[]{:S(2)}) collective-permute-start(bf16[1056,256]{1,0:T(8,128)(2,1)S(1)} %collective-permute-done.1.refs_1_), channel_id=1, source_target_pairs={{1,2},{2,3},{5,6},{6,7},{16,17},{19,20},{20,21},{23,16},{33,34},{3... | collective-permute-start | bytes 1622024 | tf_op jit(solution)/shard_map/ring_matrix/ppermute | solution.py:202
  34.8 13.1 %collective-permute-start.9 = (bf16[1040,256]{1,0:T(8,128)(2,1)S(1)}, bf16[1040,256]{1,0:T(8,128)(2,1)S(1)}, u32[]{:S(2)}, u32[]{:S(2)}) collective-permute-start(bf16[1040,256]{1,0:T(8,128)(2,1)S(1)} %collective-permute-done.8.refs_9_), channel_id=1, source_target_pairs={{32,64},{33,65},{34,66},{35,67},{36,68},{37,69},{38,70},{39,71},{4... | collective-permute-start | bytes 1597448 | tf_op jit(solution)/shard_map/ring_square/ppermute | solution.py:197
  35.5 15.0 %collective-permute-start.14 = (bf16[1040,256]{1,0:T(8,128)(2,1)S(1)}, bf16[1040,256]{1,0:T(8,128)(2,1)S(1)}, u32[]{:S(2)}, u32[]{:S(2)}) collective-permute-start(bf16[1040,256]{1,0:T(8,128)(2,1)S(1)} %collective-permute-done.12), channel_id=1, source_target_pairs={{32,64},{33,65},{34,66},{35,67},{36,68},{37,69},{38,70},{39,71},{4... | collective-permute-start | bytes 1597448 | tf_op jit(solution)/shard_map/ring_square/ppermute | solution.py:199
  40.9 12.4 %collective-permute-start.6 = (bf16[1056,256]{1,0:T(8,128)(2,1)S(1)}, bf16[1056,256]{1,0:T(8,128)(2,1)S(1)}, u32[]{:S(2)}, u32[]{:S(2)}) collective-permute-start(bf16[1056,256]{1,0:T(8,128)(2,1)S(1)} %collective-permute-done.5.refs_7_), channel_id=1, source_target_pairs={{0,7},{3,2},{4,3},{7,6},{17,16},{18,17},{21,20},{22,21},{32,39},{3... | collective-permute-start | bytes 1622024 | tf_op jit(solution)/shard_map/ring_matrix/ppermute | solution.py:205
  46.5 12.5 %collective-permute-start.3 = (bf16[1056,256]{1,0:T(8,128)(2,1)S(1)}, bf16[1056,256]{1,0:T(8,128)(2,1)S(1)}, u32[]{:S(2)}, u32[]{:S(2)}) collective-permute-start(bf16[1056,256]{1,0:T(8,128)(2,1)S(1)} %collective-permute-done.2.refs_2_), channel_id=1, source_target_pairs={{2,3},{3,4},{6,7},{7,0},{16,17},{17,18},{20,21},{21,22},{34,35},{3... | collective-permute-start | bytes 1622024 | tf_op jit(solution)/shard_map/ring_matrix/ppermute | solution.py:202
  47.8 13.1 %collective-permute-start.10 = (bf16[1040,256]{1,0:T(8,128)(2,1)S(1)}, bf16[1040,256]{1,0:T(8,128)(2,1)S(1)}, u32[]{:S(2)}, u32[]{:S(2)}) collective-permute-start(bf16[1040,256]{1,0:T(8,128)(2,1)S(1)} %collective-permute-done.9.refs_10_), channel_id=1, source_target_pairs={{16,120},{17,121},{18,122},{19,123},{20,124},{21,125},{22,126},{23... | collective-permute-start | bytes 1597448 | tf_op jit(solution)/shard_map/ring_square/ppermute | solution.py:197
  49.1 16.2 %collective-permute-start.13 = (bf16[1040,256]{1,0:T(8,128)(2,1)S(1)}, bf16[1040,256]{1,0:T(8,128)(2,1)S(1)}, u32[]{:S(2)}, u32[]{:S(2)}) collective-permute-start(bf16[1040,256]{1,0:T(8,128)(2,1)S(1)} %collective-permute-done.12), channel_id=1, source_target_pairs={{16,0},{17,1},{18,2},{19,3},{20,4},{21,5},{22,6},{23,7},{32,48},{3... | collective-permute-start | bytes 1597448 | tf_op jit(solution)/shard_map/ring_square/ppermute | solution.py:200
  50.5 15.6 %collective-permute-start.16 = (bf16[1040,256]{1,0:T(8,128)(2,1)S(1)}, bf16[1040,256]{1,0:T(8,128)(2,1)S(1)}, u32[]{:S(2)}, u32[]{:S(2)}) collective-permute-start(bf16[1040,256]{1,0:T(8,128)(2,1)S(1)} %collective-permute-done.14), channel_id=1, source_target_pairs={{16,120},{17,121},{18,122},{19,123},{20,124},{21,125},{22,126},{23... | collective-permute-start | bytes 1597448 | tf_op jit(solution)/shard_map/ring_square/ppermute | solution.py:199
  53.3 20.0 %collective-permute-start.7 = (bf16[1056,256]{1,0:T(8,128)(2,1)S(1)}, bf16[1056,256]{1,0:T(8,128)(2,1)S(1)}, u32[]{:S(2)}, u32[]{:S(2)}) collective-permute-start(bf16[1056,256]{1,0:T(8,128)(2,1)S(1)} %collective-permute-done.6.refs_6_), channel_id=1, source_target_pairs={{2,1},{3,2},{6,5},{7,6},{16,23},{17,16},{20,19},{21,20},{34,33},{3... | collective-permute-start | bytes 1622024 | tf_op jit(solution)/shard_map/ring_matrix/ppermute | solution.py:205
  59.0 14.3 %collective-permute-start.4 = (bf16[1056,256]{1,0:T(8,128)(2,1)S(1)}, bf16[1056,256]{1,0:T(8,128)(2,1)S(1)}, u32[]{:S(2)}, u32[]{:S(2)}) collective-permute-start(bf16[1056,256]{1,0:T(8,128)(2,1)S(1)} %collective-permute-done.3.refs_3_), channel_id=1, source_target_pairs={{0,1},{3,4},{4,5},{7,0},{17,18},{18,19},{21,22},{22,23},{32,33},{3... | collective-permute-start | bytes 1622024 | tf_op jit(solution)/shard_map/ring_matrix/ppermute | solution.py:202
  60.9 12.4 %collective-permute-start.11 = (bf16[1040,256]{1,0:T(8,128)(2,1)S(1)}, bf16[1040,256]{1,0:T(8,128)(2,1)S(1)}, u32[]{:S(2)}, u32[]{:S(2)}) collective-permute-start(bf16[1040,256]{1,0:T(8,128)(2,1)S(1)} %collective-permute-done.10.refs_11_), channel_id=1, source_target_pairs={{0,32},{1,33},{2,34},{3,35},{4,36},{5,37},{6,38},{7,39},{16,120},{... | collective-permute-start | bytes 1597448 | tf_op jit(solution)/shard_map/ring_square/ppermute | solution.py:197
  65.3 8.0 %collective-permute-start.15 = (bf16[1040,256]{1,0:T(8,128)(2,1)S(1)}, bf16[1040,256]{1,0:T(8,128)(2,1)S(1)}, u32[]{:S(2)}, u32[]{:S(2)}) collective-permute-start(bf16[1040,256]{1,0:T(8,128)(2,1)S(1)} %collective-permute-done.14), channel_id=1, source_target_pairs={{64,80},{65,81},{66,82},{67,83},{68,84},{69,85},{70,86},{71,87},{8... | collective-permute-start | bytes 1597448 | tf_op jit(solution)/shard_map/ring_square/ppermute | solution.py:200
  66.0 7.3 %collective-permute-start.17 = (bf16[1040,256]{1,0:T(8,128)(2,1)S(1)}, bf16[1040,256]{1,0:T(8,128)(2,1)S(1)}, u32[]{:S(2)}, u32[]{:S(2)}) collective-permute-start(bf16[1040,256]{1,0:T(8,128)(2,1)S(1)} %collective-permute-done.16), channel_id=1, source_target_pairs={{0,16},{1,17},{2,18},{3,19},{4,20},{5,21},{6,22},{7,23},{48,32},{4... | collective-permute-start | bytes 1597448 | tf_op jit(solution)/shard_map/ring_square/ppermute | solution.py:200
  76.1 3.8 %collective-permute-start.18 = (f32[8,2,32,256]{3,2,1,0:T(8,128)S(1)}, f32[8,2,32,256]{3,2,1,0:T(8,128)S(1)}, u32[]{:S(2)}, u32[]{:S(2)}) collective-permute-start(f32[8,2,32,256]{3,2,1,0:T(8,128)S(1)} %get-tuple-element.8), channel_id=1, source_target_pairs={{0,16},{1,17},{2,18},{3,19},{4,20},{5,21},{6,22},{7,23},{16,0},{17... | collective-permute-start | bytes 1572872 | tf_op jit(solution)/shard_map/pair_sum/ppermute | solution.py:210
